TPU v7x, 512 devices: a whole 4x8x8 slice. The times are simulated.
512 devices in a mesh: lat: 64 (over y, x, z_lo), lon: 8 (over z_hi, core).
Axes of the slice: x: 4, y: 8, z: 8 (z_hi: 4, z_lo: 2; z = z_hi * 2 + z_lo), core: 2. Of those that a mesh axis runs over, the one named last changes fastest.
Arguments:
- grid_state: bfloat16 [2, 384, 192, 192], P(None, 'lat', 'lon'), may hold values from -20 to 20
- cotangent: bfloat16 [2, 384, 192, 192], P(None, 'lat', 'lon'), may hold values from -6 to 6
- mask_ids: int32 [2, 384, 192], P(None, 'lat', 'lon'), may hold values from 0 to 2
- earth_bias: float32 [2, 6, 12, 12, 23], replicated, may hold values from -6 to 360
- qkv_weight: bfloat16 [192, 576], replicated, may hold values from -0.4375 to 0.4375
- proj_weight: bfloat16 [192, 192], replicated, may hold values from -0.4375 to 0.4375
Outputs:
- grad_field: bfloat16 [2, 384, 192, 192], P(None, 'lat', 'lon')
- grad_qkv: float32 [192, 576], replicated
- grad_proj: float32 [192, 192], replicated
- grad_bias: float32 [2, 6, 12, 12, 23], replicated
Inputs may be any that keep to these rules, and one draw needn't show every extreme that they name: `mask_ids`: cells of different mask ids do not attend to each other.
All inputs are finite; a program needn't handle non-finite values.
Results may differ from a plain program's by a relative error of at most 0.011.
Values may be sent and summed in bfloat16 or wider, within the bound.
A program may use at most 64 MiB of HBM per device.

v0:
```python
import jax
import jax.numpy as jnp
from jax import lax
from jax.sharding import PartitionSpec as P

LAT_GROUP = 2


def passed_along(block, axis, distance):
    devices = range(lax.axis_size(axis))
    route = [((i - distance) % len(devices), i) for i in devices]
    return lax.ppermute(block, axis, route)


def swapped(array, axis, stride):
    return lax.ppermute(array, axis, [(i, i ^ 1 << stride) for i in range(lax.axis_size(axis))])


def offset_table():
    places = jnp.arange(12, dtype=jnp.int32)
    spread = places[:, None] - places[None, :] + 11
    return (spread[:, :, None] == jnp.arange(23, dtype=jnp.int32)[None, None, :]).astype(
        jnp.float32
    )


def window_grad(
    grid_block, cot_block, id_block, region, bias_block, qkv_weight, proj_weight, offsets
):
    levels, rows_dev, cols_dev, width = grid_block.shape
    lat_windows = rows_dev // 6
    longitude_window_count = cols_dev // 12
    head_count = bias_block.shape[1]
    head_size = width // head_count
    win_size = levels * 72
    score_scale = head_size ** (-0.5)

    def to_windows(tensor):
        last_dim = tensor.shape[-1]
        shaped = tensor.reshape(levels, lat_windows, 6, longitude_window_count, 12, last_dim)
        return shaped.transpose(1, 3, 0, 2, 4, 5).reshape(
            lat_windows, longitude_window_count, win_size, last_dim
        )

    def from_windows(tensor):
        last_dim = tensor.shape[-1]
        shaped = tensor.reshape(lat_windows, longitude_window_count, levels, 6, 12, last_dim)
        return shaped.transpose(2, 0, 3, 1, 4, 5).reshape(levels * rows_dev * cols_dev, last_dim)

    inputs = grid_block.astype(jnp.float32).reshape(-1, width)
    mean_removed = inputs - jnp.mean(inputs, axis=-1, keepdims=True)
    reciprocal_deviation = lax.rsqrt(
        jnp.mean(mean_removed * mean_removed, axis=-1, keepdims=True) + 1e-05
    )
    standardized_input = mean_removed * reciprocal_deviation
    normalized_input = standardized_input.astype(jnp.bfloat16)
    projected = jnp.dot(normalized_input, qkv_weight, preferred_element_type=jnp.float32).astype(
        jnp.bfloat16
    )
    split_win = to_windows(projected).reshape(
        lat_windows, longitude_window_count, win_size, 3, head_count, head_size
    )
    queries = split_win[:, :, :, 0]
    keys_win = split_win[:, :, :, 1]
    values_win = split_win[:, :, :, 2]
    full_bias = jnp.einsum(
        "rhabo,xyo->rhaxby", bias_block, offsets, precision=lax.Precision.HIGHEST
    )
    full_bias = full_bias.reshape(lat_windows, head_count, win_size, win_size)
    id_win = to_windows(id_block.reshape(-1, 1))[..., 0]
    region_tok = jnp.broadcast_to(region[None, :, None], (levels, rows_dev, cols_dev)).reshape(
        -1, 1
    )
    region_win = to_windows(region_tok)[..., 0]
    allowed = (id_win[..., :, None] == id_win[..., None, :]) & (
        region_win[..., :, None] == region_win[..., None, :]
    )
    scores = (
        jnp.einsum("rnqhd,rnkhd->rnhqk", queries, keys_win, preferred_element_type=jnp.float32)
        * score_scale
    )
    scores = scores + full_bias[:, None]
    scores = jnp.where(allowed[:, :, None], scores, -jnp.inf)
    row_max = jnp.max(scores, axis=-1, keepdims=True)
    exponent = jnp.exp(scores - row_max)
    softmaxed = exponent / jnp.sum(exponent, axis=-1, keepdims=True)
    soft_bf = softmaxed.astype(jnp.bfloat16)
    attended = jnp.einsum(
        "rnhqk,rnkhd->rnqhd", soft_bf, values_win, preferred_element_type=jnp.float32
    ).astype(jnp.bfloat16)
    att_tokens = from_windows(
        attended.reshape(lat_windows, longitude_window_count, win_size, width)
    )
    cot_tokens = cot_block.reshape(-1, width)
    grad_proj = jnp.dot(att_tokens.T, cot_tokens, preferred_element_type=jnp.float32)
    d_att = jnp.dot(cot_tokens, proj_weight.T, preferred_element_type=jnp.float32).astype(
        jnp.bfloat16
    )
    d_att = to_windows(d_att).reshape(
        lat_windows, longitude_window_count, win_size, head_count, head_size
    )
    d_value = jnp.einsum(
        "rnhqk,rnqhd->rnkhd", soft_bf, d_att, preferred_element_type=jnp.float32
    ).astype(jnp.bfloat16)
    d_prob = jnp.einsum("rnqhd,rnkhd->rnhqk", d_att, values_win, preferred_element_type=jnp.float32)
    d_score = softmaxed * (d_prob - jnp.sum(softmaxed * d_prob, axis=-1, keepdims=True))
    band_sum = jnp.sum(d_score, axis=1).reshape(
        lat_windows, head_count, levels * 6, 12, levels * 6, 12
    )
    grad_bias = jnp.einsum("rhaxby,xyo->rhabo", band_sum, offsets, precision=lax.Precision.HIGHEST)
    score_bf = d_score.astype(jnp.bfloat16)
    d_query = (
        jnp.einsum("rnhqk,rnkhd->rnqhd", score_bf, keys_win, preferred_element_type=jnp.float32)
        * score_scale
    ).astype(jnp.bfloat16)
    d_key = (
        jnp.einsum("rnhqk,rnqhd->rnkhd", score_bf, queries, preferred_element_type=jnp.float32)
        * score_scale
    ).astype(jnp.bfloat16)
    d_qkv = jnp.stack([d_query, d_key, d_value], axis=3).reshape(
        lat_windows, longitude_window_count, win_size, 3 * width
    )
    d_qkv = from_windows(d_qkv)
    grad_qkv = jnp.dot(normalized_input.T, d_qkv, preferred_element_type=jnp.float32)
    normalized_gradient = jnp.dot(d_qkv, qkv_weight.T, preferred_element_type=jnp.float32)
    mean_removed_gradient = (
        normalized_gradient
        - jnp.mean(normalized_gradient, axis=-1, keepdims=True)
        - standardized_input
        * jnp.mean(normalized_gradient * standardized_input, axis=-1, keepdims=True)
    )
    grad_field = cot_tokens.astype(jnp.float32) + reciprocal_deviation * mean_removed_gradient
    return (
        grad_field.astype(jnp.bfloat16).reshape(grid_block.shape),
        grad_qkv,
        grad_proj,
        grad_bias,
    )


def body(grid_state, cotangent, mask_ids, earth_bias, qkv_weight, proj_weight):
    levels, rows_dev, cols_dev, width = grid_state.shape
    id_values = mask_ids.astype(jnp.bfloat16)
    own_arrays = (grid_state, cotangent, id_values)
    east_parts = passed_along(
        (grid_state[:, :, :6], cotangent[:, :, :6], id_values[:, :, :6]), "lon", -1
    )
    widened = [
        jnp.concatenate([own_block, edge_part], axis=2)
        for own_block, edge_part in zip(own_arrays, east_parts)
    ]
    position = lax.axis_index("lat") % LAT_GROUP
    on_last = position == LAT_GROUP - 1
    north_parts = swapped((widened[0][:, :3], widened[1][:, :3], widened[2][:, :3]), "lat", 0)
    blocks = [
        jnp.concatenate([own_block[:, 3:], edge_part], axis=1)[:, :, 6:]
        for own_block, edge_part in zip(widened, north_parts)
    ]
    row_index = jnp.arange(rows_dev, dtype=jnp.int32)
    region = jnp.where(on_last & (row_index >= rows_dev - 3), 1, 0).astype(jnp.int32)
    band_count = rows_dev // 6
    band_start = position * band_count
    local_bias = lax.dynamic_slice_in_dim(earth_bias, band_start, band_count, 0)
    grad_block, grad_qkv, grad_proj, grad_bias = window_grad(
        blocks[0], blocks[1], blocks[2], region, local_bias, qkv_weight, proj_weight, offset_table()
    )
    padded = (
        jnp.zeros((levels, rows_dev + 3, cols_dev + 6, width), jnp.bfloat16)
        .at[:, 3:, 6:]
        .set(grad_block)
    )
    tail_rows = padded[:, rows_dev:]
    returned = swapped(tail_rows, "lat", 0)
    own_frame = jnp.concatenate([returned, padded[:, 3:rows_dev]], axis=1)
    east_back = passed_along(own_frame[:, :, cols_dev:], "lon", 1)
    grad_field = jnp.concatenate([east_back, own_frame[:, :, 6:cols_dev]], axis=2)
    token_count_overall = levels * rows_dev * cols_dev * lax.axis_size("lat") * lax.axis_size("lon")
    token_scale = token_count_overall ** (-0.5)
    placed = lax.dynamic_update_slice_in_dim(
        jnp.zeros(earth_bias.shape, jnp.float32), grad_bias, band_start, 0
    )
    total_qkv, total_proj, total_bias = lax.psum((grad_qkv, grad_proj, placed), ("lat", "lon"))
    return (grad_field, total_qkv * token_scale, total_proj * token_scale, total_bias)


def solution(mesh):
    placed = (
        P(None, "lat", "lon", None),
        P(None, "lat", "lon", None),
        P(None, "lat", "lon"),
        P(),
        P(),
        P(),
    )
    return jax.shard_map(
        body,
        mesh=mesh,
        in_specs=placed,
        out_specs=(P(None, "lat", "lon", None), P(), P(), P()),
        check_vma=False,
    )
```

profile of v0, /device:TPU:1, one launch (start us, length us, event | category | flops | bytes accessed | tf_op | source)
XLA Modules:
  0.0 402.2 jit_solution(13862793517713691259)
XLA Ops:
  7.2 0.8 convert_element_type.75
  8.0 8.8 %collective-permute-start.4 = (bf16[2,6,6]{2,0,1:T(2,128)(2,1)S(1)}, bf16[2,6,6]{2,0,1:T(2,128)(2,1)S(1)}, u32[]{:S(2)}, u32[]{:S(2)}) collective-permute-start(bf16[2,6,6]{2,0,1:T(2,128)(2,1)S(1)} %bitcast.131), channel_id=1, source_target_pairs={{1,0},{2,1},{3,2},{4,3},{5,4},{6,5},{7,6},{0,7},{9,8},{10,9},{11,1... | collective-permute-start | bytes 440 | tf_op jit(solution)/shard_map/ppermute | solution.py:12
  16.8 0.8 slice.93
  17.6 5.0 %collective-permute-start.2 = (bf16[2,6,6,192]{3,2,1,0:T(8,128)(2,1)S(1)}, bf16[2,6,6,192]{3,2,1,0:T(8,128)(2,1)S(1)}, u32[]{:S(2)}, u32[]{:S(2)}) collective-permute-start(bf16[2,6,6,192]{3,2,1,0:T(8,128)(2,1)S(1)} %slice.93), channel_id=1, source_target_pairs={{1,0},{2,1},{3,2},{4,3},{5,4},{6,5},{7,6},{0,7},{9,8},{10,9},{11,1... | collective-permute-start | bytes 82952 | tf_op jit(solution)/shard_map/ppermute | solution.py:12
  22.6 0.8 slice.89
  23.4 2.6 collective-permute-start
  26.0 0.9 constant_dynamic-update-slice_fusion.3
  27.5 5.0 %convolution_bitcast_fusion = f32[1,6,12,12,12,12]{4,5,2,1,3,0:T(8,128)} fusion(f32[1,6,12,12,23]{4,0,3,2,1:T(1,128)S(1)} %constant_dynamic-slice_fusion, s32[12,12]{1,0:T(8,128)S(1)} %subtract_add_fusion), kind=kOutput, calls=%fused_computation.1 | convolution fusion | flops 34342128 | bytes 577728 | tf_op jit(solution)/shard_map/rhabo,xyo->rhaxby/dot_general | solution.py:66
  32.7 3.1 collective-permute-start.5
  35.8 11.7 %copy.65 = f32[1,6,12,12,12,12]{3,2,5,4,1,0:T(8,128)} copy(f32[1,6,12,12,12,12]{4,5,2,1,3,0:T(8,128)} %convolution_bitcast_fusion) | data formatting | bytes 995328 | tf_op jit(solution)/shard_map/add | solution.py:82
  47.4 5.7 %reshape.263 = f32[6,144,144]{1,2,0:T(8,128)} reshape(f32[1,6,12,12,12,12]{3,2,5,4,1,0:T(8,128)} %copy.65) | data formatting | bytes 995328 | tf_op jit(solution)/shard_map/add | solution.py:82
  53.6 0.8 compare_and_fusion
  54.4 2.2 collective-permute-start.3
  56.6 0.7 fusion.45
  57.3 3.1 collective-permute-start.1
  62.2 1.6 reshape_reshape.14
  63.8 1.3 fusion.43
  65.2 1.5 copy.67
  66.7 2.1 copy.68
  68.8 1.1 copy.70
  69.9 0.9 pad_maximum_fusion.2
  71.6 1.1 copy.45
  72.7 2.1 fusion.46
  74.8 2.3 fusion.4
  77.0 0.5 multiply_reduce_fusion
  77.5 2.1 fusion.7
  80.3 0.8 copy-done.5
  81.5 5.0 %reshape.259 = f32[6,12,12,12,12]{2,1,4,3,0:T(8,128)} reshape(f32[6,144,144]{1,2,0:T(8,128)S(1)} %get-tuple-element.21) | data formatting | bytes 995328 | tf_op jit(solution)/shard_map/reshape.86
  86.5 6.0 %fusion.27 = f32[6,12,12,23,1]{3,1,4,2,0:T(8,128)S(1)} fusion(f32[6,12,12,12,12]{2,1,4,3,0:T(8,128)} %reshape.259, pred[12,12,23,1,1]{2,1,0,3,4:T(8,128)(4,1)S(1)} %fusion.25), kind=kOutput, calls=%fused_computation.56 | convolution fusion | flops 34338816 | bytes 580464 | tf_op jit(solution)/shard_map/rhaxby,xyo->rhabo/dot_general | solution.py:110
  92.6 1.2 copy.56
  93.9 0.5 copy.53
  94.8 0.9 fusion.52
  95.7 0.9 pad_maximum_fusion
  96.7 2.0 copy.50
  98.7 2.4 reshape_reshape.16
  101.1 1.0 copy.51
  102.9 1.1 fusion.51
  104.3 9.3 %dynamic_update_slice.3 = f32[2,6,12,12,23]{4,0,3,2,1:T(2,128)S(1)} dynamic-update-slice(f32[2,6,12,12,23]{4,0,3,2,1:T(2,128)S(1)} %broadcast_in_dim.26, f32[1,6,12,12,23]{4,0,3,2,1:T(1,128)S(1)} %copy-done.3, s32[]{:T(128)S(6)} %select_n.26, s32[]{:T(128)} %constant.67.clone.1, s32[]{:T(128)} %constant.67.clone.1, s32[]{:T(128)} %constant.67.clone.1, s32[]{:T(128)} %constant.67.clone.1) | dynamic-update-slice | bytes 158980 | tf_op jit(solution)/shard_map/dynamic_update_slice | solution.py:179
  113.6 0.9 copy-done.1
  114.9 2.2 collective-permute-start.6
  117.0 3.2 collective-permute-done.6
  120.2 6.1 %collective-permute-start.7 = (bf16[2,6,6,192]{3,2,1,0:T(8,128)(2,1)S(1)}, bf16[2,6,6,192]{3,2,1,0:T(8,128)(2,1)S(1)}, u32[]{:S(2)}, u32[]{:S(2)}) collective-permute-start(bf16[2,6,6,192]{3,2,1,0:T(8,128)(2,1)S(1)} %pad_maximum_fusion.3), channel_id=1, source_target_pairs={{7,0},{0,1},{1,2},{2,3},{3,4},{4,5},{5,6},{6,7},{15,8},{8,9},{9,10... | collective-permute-start | bytes 82952 | tf_op jit(solution)/shard_map/ppermute | solution.py:12
  126.4 1.2 collective-permute-done.7
  127.5 0.7 fusion.22
  128.2 262.7 %all-reduce.4.cloned.1.call-done = (f32[192,576]{1,0:T(8,128)}, f32[192,192]{1,0:T(8,128)}, f32[2,6,12,12,23]{4,0,3,2,1:T(2,128)}) async-done(((f32[192,576]{1,0:T(8,128)}, f32[192,192]{1,0:T(8,128)}, f32[2,6,12,12,23]{4,0,3,2,1:T(2,128)}), (f32[192,576]{1,0:T(8,128)}, f32[192,192]{1,0:T(8,128)}, f32[2,6,12,12,23]{4,0,3,2,1:T(2,128)})) %all-reduce.4.cloned.1.call-update) | async-done | bytes 748816 | tf_op jit(solution)/shard_map/psum | solution.py:182
  390.9 1.9 broadcast_multiply_fusion
  392.8 1.6 broadcast_multiply_fusion.1
  394.5 0.9 copy.85
  (90 shorter events, 6.6 us)
Async XLA Ops:
  7.2 19.9 %copy-start = (f32[2,6,12,12,23]{4,0,3,2,1:T(2,128)S(1)}, f32[2,6,12,12,23]{4,0,3,2,1:T(2,128)}, u32[]{:S(2)}) copy-start(f32[2,6,12,12,23]{4,0,3,2,1:T(2,128)} %param.11) | copy-start | bytes 476932
  7.2 383.7 %all-reduce.4.cloned.1.call-start = ((), (), s32[]{:S(2)}) async-start(), calls=%async_computation | async-start | bytes 3145728 | tf_op jit(solution)/shard_map/psum | solution.py:182
  8.0 24.6 %collective-permute-start.4 = (bf16[2,6,6]{2,0,1:T(2,128)(2,1)S(1)}, bf16[2,6,6]{2,0,1:T(2,128)(2,1)S(1)}, u32[]{:S(2)}, u32[]{:S(2)}) collective-permute-start(bf16[2,6,6]{2,0,1:T(2,128)(2,1)S(1)} %bitcast.131), channel_id=1, source_target_pairs={{1,0},{2,1},{3,2},{4,3},{5,4},{6,5},{7,6},{0,7},{9,8},{10,9},{11,1... | collective-permute-start | bytes 440 | tf_op jit(solution)/shard_map/ppermute | solution.py:12
  17.6 36.8 %collective-permute-start.2 = (bf16[2,6,6,192]{3,2,1,0:T(8,128)(2,1)S(1)}, bf16[2,6,6,192]{3,2,1,0:T(8,128)(2,1)S(1)}, u32[]{:S(2)}, u32[]{:S(2)}) collective-permute-start(bf16[2,6,6,192]{3,2,1,0:T(8,128)(2,1)S(1)} %slice.93), channel_id=1, source_target_pairs={{1,0},{2,1},{3,2},{4,3},{5,4},{6,5},{7,6},{0,7},{9,8},{10,9},{11,1... | collective-permute-start | bytes 82952 | tf_op jit(solution)/shard_map/ppermute | solution.py:12
  23.4 33.2 %collective-permute-start = (bf16[2,6,6,192]{3,2,1,0:T(8,128)(2,1)S(1)}, bf16[2,6,6,192]{3,2,1,0:T(8,128)(2,1)S(1)}, u32[]{:S(2)}, u32[]{:S(2)}) collective-permute-start(bf16[2,6,6,192]{3,2,1,0:T(8,128)(2,1)S(1)} %slice.89), channel_id=1, source_target_pairs={{1,0},{2,1},{3,2},{4,3},{5,4},{6,5},{7,6},{0,7},{9,8},{10,9},{11,1... | collective-permute-start | bytes 82952 | tf_op jit(solution)/shard_map/ppermute | solution.py:12
  27.5 5.0 %copy-start.11 = (bf16[2,6,24,192]{3,2,1,0:T(8,128)(2,1)S(1)}, bf16[2,6,24,192]{3,2,1,0:T(8,128)(2,1)}, u32[]{:S(2)}) copy-start(bf16[2,6,24,192]{3,2,1,0:T(8,128)(2,1)} %param.9) | copy-start | bytes 331780
  32.7 20.7 %collective-permute-start.5 = (bf16[2,3,30]{2,0,1:T(2,128)(2,1)S(1)}, bf16[2,3,30]{2,0,1:T(2,128)(2,1)S(1)}, u32[]{:S(2)}, u32[]{:S(2)}) collective-permute-start(bf16[2,3,30]{2,0,1:T(2,128)(2,1)S(1)} %get-tuple-element.33), channel_id=1, source_target_pairs={{0,8},{8,0},{16,24},{24,16},{32,40},{40,32},{48,56},{56,48},{64,72... | collective-permute-start | bytes 1088 | tf_op jit(solution)/shard_map/ppermute | solution.py:16
  53.1 8.4 %copy-start.6 = (bf16[192,576]{1,0:T(8,128)(2,1)S(1)}, bf16[192,576]{1,0:T(8,128)(2,1)}, u32[]{:S(2)}) copy-start(bf16[192,576]{1,0:T(8,128)(2,1)} %param.12) | copy-start | bytes 663556
  54.4 6.0 %collective-permute-start.3 = (bf16[2,3,30,192]{3,2,1,0:T(8,128)(2,1)S(1)}, bf16[2,3,30,192]{3,2,1,0:T(8,128)(2,1)S(1)}, u32[]{:S(2)}, u32[]{:S(2)}) collective-permute-start(bf16[2,3,30,192]{3,2,1,0:T(8,128)(2,1)S(1)} %get-tuple-element.27), channel_id=1, source_target_pairs={{0,8},{8,0},{16,24},{24,16},{32,40},{40,32},{48,56},{56,48},{64,72... | collective-permute-start | bytes 207368 | tf_op jit(solution)/shard_map/ppermute | solution.py:16
  57.3 12.6 %collective-permute-start.1 = (bf16[2,3,30,192]{3,2,1,0:T(8,128)(2,1)}, bf16[2,3,30,192]{3,2,1,0:T(8,128)(2,1)}, u32[]{:S(2)}, u32[]{:S(2)}) collective-permute-start(bf16[2,3,30,192]{3,2,1,0:T(8,128)(2,1)} %get-tuple-element.29), channel_id=1, source_target_pairs={{0,8},{8,0},{16,24},{24,16},{32,40},{40,32},{48,56},{56,48},{64,72... | collective-permute-start | bytes 207368 | tf_op jit(solution)/shard_map/ppermute | solution.py:16
  60.6 0.6 copy-start.16
  60.9 0.6 copy-start.18
  65.1 3.6 copy-start.2
  65.2 4.7 %copy-start.10 = (bf16[2,3,30,192]{3,2,1,0:T(8,128)(2,1)S(1)}, bf16[2,3,30,192]{3,2,1,0:T(8,128)(2,1)}, u32[]{:S(2)}) copy-start(bf16[2,3,30,192]{3,2,1,0:T(8,128)(2,1)} %get-tuple-element.28) | copy-start | bytes 207364
  65.2 5.7 %copy-start.15 = (bf16[192,192]{1,0:T(8,128)(2,1)S(1)}, bf16[192,192]{1,0:T(8,128)(2,1)}, u32[]{:S(2)}) copy-start(bf16[192,192]{1,0:T(8,128)(2,1)} %param.13) | copy-start | bytes 221188
  74.7 2.3 copy-start.4
  74.7 2.3 copy-start.13
  74.7 2.3 copy-start.14
  77.5 2.4 copy-start.9
  79.6 1.5 copy-start.5
  92.5 1.4 copy-start.12
  98.7 3.6 copy-start.7
  102.3 2.0 copy-start.3
  104.0 10.5 %copy-start.17 = (f32[288]{0:T(512)S(1)}, f32[288]{0:T(512)}, u32[]{:S(2)}) copy-start(f32[288]{0:T(512)} %copy-done.16) | copy-start | bytes 3460
  104.0 10.5 %copy-start.19 = (f32[288]{0:T(512)S(1)}, f32[288]{0:T(512)}, u32[]{:S(2)}) copy-start(f32[288]{0:T(512)} %copy-done.18) | copy-start | bytes 3460
  113.6 0.9 copy-start.1
  114.9 5.4 %collective-permute-start.6 = (bf16[2,3,30,192]{3,2,1,0:T(8,128)(2,1)S(1)}, bf16[2,3,30,192]{3,2,1,0:T(8,128)(2,1)S(1)}, u32[]{:S(2)}, u32[]{:S(2)}) collective-permute-start(bf16[2,3,30,192]{3,2,1,0:T(8,128)(2,1)S(1)} %get-tuple-element.30), channel_id=1, source_target_pairs={{0,8},{8,0},{16,24},{24,16},{32,40},{40,32},{48,56},{56,48},{64,72... | collective-permute-start | bytes 207368 | tf_op jit(solution)/shard_map/ppermute | solution.py:16
  120.2 7.3 %collective-permute-start.7 = (bf16[2,6,6,192]{3,2,1,0:T(8,128)(2,1)S(1)}, bf16[2,6,6,192]{3,2,1,0:T(8,128)(2,1)S(1)}, u32[]{:S(2)}, u32[]{:S(2)}) collective-permute-start(bf16[2,6,6,192]{3,2,1,0:T(8,128)(2,1)S(1)} %pad_maximum_fusion.3), channel_id=1, source_target_pairs={{7,0},{0,1},{1,2},{2,3},{3,4},{4,5},{5,6},{6,7},{15,8},{8,9},{9,10... | collective-permute-start | bytes 82952 | tf_op jit(solution)/shard_map/ppermute | solution.py:12
  390.9 3.6 copy-start.8
Sparse Core Ops, SparseCore 0:
  114.7 276.2 all-reduce.3
where the time goes:
time: 404 us; the launch traced here: 402 us
  waiting for transfers between devices  267 us (66%)
  local copies, waits for them, and re-layouts  56.8 us (14%)
  starting transfers between devices  33 us (8%)
  matrix products  19.8 us (5%)
  between operations  14.6 us (4%)
  other arithmetic  10.9 us (3%)
    psum x1, waiting for transfers between devices, body(): lax.psum((grad_qkv, grad_proj, placed), ('lat', 'lon'))  263 us
    ppermute x4, starting transfers between devices, passed_along(): return lax.ppermute(block, axis, route)  22.5 us
    add x2, local copies, waits for them, and re-layouts, window_grad(): scores = scores + full_bias[:, None]  17.4 us
    ppermute x4, starting transfers between devices, swapped(): lax.ppermute(array, axis, [(i, i ^ 1 << stride) for i in range(lax.axis_s...  10.5 us
    dynamic_update_slice x1, local copies, waits for them, and re-layouts, body(): lax.dynamic_update_slice_in_dim(jnp.zeros(earth_bias.shape, jnp.float32),...  9.31 us
    unnamed x46, local copies, waits for them, and re-layouts  8.81 us
  transfers between devices with their start and end apart: 9, of which 3 were waited for; matrix products, arithmetic and copies ran while one was open for 9% of the time, Pallas kernels for 0%

commit v1 on v0

v1 whole, which is shorter than its diff:
```python
import functools

import jax
import jax.numpy as jnp
import numpy as np
from jax import lax
from jax.experimental import pallas as pl
from jax.experimental.pallas import tpu as pltpu
from jax.sharding import PartitionSpec as P

MESH = pl.DeviceIdType.MESH
F32, BF16 = jnp.float32, jnp.bfloat16

TOK = 288
WIN = 144
WIDTH = 192
HEADS = 6
OWN, EAST, SWAP, CORNER, ALL = 0, 288, 336, 448, 496
CHUNKS, TILES = 8, 7
HALF = 51
ROWS_MAIN, COLS_MAIN = 12, 6
BIAS_TILES = 15


def build_tables():
    natural = lambda z, r, c: (z * 6 + r) * 24 + c
    send = np.zeros((208, TOK), np.float32)
    for z in range(2):
        for r in range(3):
            for c in range(6):
                send[(z * 3 + r) * 6 + c, natural(z, r + 3, c)] = 1
                send[160 + (z * 3 + r) * 6 + c, natural(z, r, c)] = 1
            for c in range(18):
                send[48 + (z * 3 + r) * 18 + c, natural(z, r, c + 6)] = 1
    frame = np.zeros((TOK, ALL), np.float32)
    id_rows = np.zeros((TOK, 64), np.float32)
    id_cols = np.zeros((TOK, 128), np.float32)
    wrapped = np.zeros((TOK, 128), np.float32)
    for w in range(2):
        for z in range(2):
            for r in range(6):
                for p in range(12):
                    t = w * WIN + (z * 6 + r) * 12 + p
                    c = w * 12 + p
                    if r < 3 and c < 18:
                        src, block, row, col = natural(z, r + 3, c + 6), 0, r + 3, c + 6
                    elif r < 3:
                        src, block, row, col = EAST + (z * 3 + r) * 6 + c - 18, 1, r + 3, c - 18
                    elif c < 18:
                        src, block, row, col = SWAP + (z * 3 + r - 3) * 18 + c, 2, r - 3, c + 6
                    else:
                        src, block, row, col = (
                            CORNER + (z * 3 + r - 3) * 6 + c - 18, 3, r - 3, c - 18)
                    frame[t, src] = 1
                    id_rows[t, block * 16 + z * 8 + row] = 1
                    id_cols[t, col] = 1
                    wrapped[t, :] = 3.0 if r >= 3 else 0.0
    back = frame[:, OWN + TOK:].T
    out = np.concatenate([frame[:, :TOK].T, send.T], axis=1)
    spread = np.zeros((384, 1792), np.float32)
    for x in range(12):
        for b in range(12):
            for y in range(12):
                key = b * 12 + y
                col = x * 128 + key if key < 128 else 1536 + x * 16 + key - 128
                spread[b * 32 + x - y + 11, col] = 1
    cells = np.concatenate([send, back], axis=0)
    moves = np.concatenate([frame, out], axis=0)
    ids = np.concatenate([id_rows, np.zeros((TOK, 64), np.float32), id_cols, wrapped], axis=1)
    return [np.asarray(t, jnp.bfloat16) for t in (cells, moves, ids, spread)]


def mm(a, b):
    return lax.dot_general(a, b, (((1,), (0,)), ((), ())), preferred_element_type=F32)


def mm_nt(a, b):
    return lax.dot_general(a, b, (((1,), (1,)), ((), ())), preferred_element_type=F32)


def mm_tn(a, b):
    return lax.dot_general(a, b, (((0,), (0,)), ((), ())), preferred_element_type=F32)


def tile_place(t):
    return t // HALF, (t % HALF) // TILES, (t % HALF) % TILES


def kernel(
    x_hbm, cot_hbm, ids_hbm, eb_hbm, wqkv_hbm, wproj_hbm, cells_hbm, moves_hbm, idt_hbm, spread_hbm,
    field_ref, gqkv_ref, gproj_ref, gbias_ref,
    x_v, cot_v, ids_v, eb_v, wqkv_v, wproj_v, cells_v, moves_v, idt_v, spread_v,
    xc, send_b, idb, e2d, fa, fb, ba, bb, gback, ret_b, gs,
    pay, rc, cur, ra, ry, rz, fin, o2d,
    in_sem, h_ss, h_rs, r_ss, r_rs, c_ss, c_rs, a_ss, a_rs, y_ss, y_rs, z_ss, z_rs,
    g_ss, g_rs, k_ss, k_rs,
):
    lat, lon = lax.axis_index("lat"), lax.axis_index("lon")
    iy, ix, izl = lat // 8, (lat // 2) % 4, lat % 2
    izh, core = lon // 2, lon % 2
    group = ix * 2 + izl
    band = izl

    lat_o = lat + 1 - 2 * izl
    east, west = (lon + 1) % 8, (lon + 7) % 8
    sibling = (lat, izh * 2 + 1 - core)

    def member(g):
        return (iy * 8 + g, lon)

    def at_y(y):
        return (y * 8 + group, lon)

    def at_zh(zh):
        return (lat, zh * 2 + core)

    barrier = pltpu.get_barrier_semaphore()
    partners = [(lat, west), (lat, east), (lat_o, lon), (lat_o, west), (lat_o, east), sibling]
    partners += [member((group + d) % 8) for d in range(1, 8)]
    partners += [at_y((iy + d) % 8) for d in range(1, 8)]
    partners += [at_zh((izh + d) % 4) for d in range(1, 4)]
    for p in partners:
        pl.semaphore_signal(barrier, inc=1, device_id=p, device_id_type=MESH)

    srcs = [x_hbm, cot_hbm, cells_hbm, ids_hbm, eb_hbm.at[band], spread_hbm, moves_hbm, idt_hbm,
            wqkv_hbm, wproj_hbm]
    dsts = [x_v, cot_v, cells_v, ids_v, eb_v, spread_v, moves_v, idt_v, wqkv_v, wproj_v]
    loads = [pltpu.make_async_copy(s, d, in_sem.at[i]) for i, (s, d) in enumerate(zip(srcs, dsts))]
    for cp in loads:
        cp.start()

    loads[0].wait()
    loads[1].wait()
    loads[2].wait()
    loads[3].wait()
    xc[0:TOK, 0:192] = x_v[...]
    xc[0:TOK, 192:384] = cot_v[...]
    send_b[...] = mm(cells_v[0:208, :], xc[0:TOK, :]).astype(BF16)
    idb[0] = jnp.zeros((16, 128), F32)
    idb[0, 0:6, 0:24] = ids_v[0].astype(F32)
    idb[0, 8:14, 0:24] = ids_v[1].astype(F32)

    pl.semaphore_wait(barrier, len(partners))

    def remote(src, dst, ss, rs, dev):
        return pltpu.make_async_remote_copy(
            src_ref=src, dst_ref=dst, send_sem=ss, recv_sem=rs, device_id=dev, device_id_type=MESH)

    strips = [(0, EAST, 48, (lat, west)), (48, SWAP, 112, (lat_o, lon)), (160, CORNER, 48, (lat_o, west))]
    halo = []
    for i, (a, b, n, dev) in enumerate(strips):
        halo.append(remote(send_b.at[pl.ds(a, n)], xc.at[pl.ds(b, n)], h_ss.at[i], h_rs.at[i], dev))
        halo.append(remote(idb.at[0], idb.at[i + 1], h_ss.at[3 + i], h_rs.at[3 + i], dev))
    for cp in halo:
        cp.start()

    loads[4].wait()
    loads[5].wait()
    e2d[...] = jnp.zeros(e2d.shape, F32)
    for h in range(HEADS):
        for a in range(12):
            r0 = (h * 12 + a) * 16
            e2d[r0:r0 + 12, 0:23] = eb_v[h, a]
    packs = []
    for g in range(3):
        acc = e2d[pl.ds(4 * g, 72, stride=16), :]
        for k in range(1, 4):
            acc = acc + pltpu.roll(e2d[pl.ds(4 * g + k, 72, stride=16), :], 32 * k, 1)
        packs.append(acc)
    e = jnp.concatenate(packs, axis=1)
    hi = e.astype(BF16)
    rest = e - hi.astype(F32)
    mid = rest.astype(BF16)
    low = (rest - mid.astype(F32)).astype(BF16)
    full = (mm(hi, spread_v[...]) + mm(mid, spread_v[...])) + mm(low, spread_v[...])
    for x in range(12):
        fa[pl.ds(x, 72, stride=12), :] = full[:, x * 128:(x + 1) * 128]
        tail = full[:, 1536 + (x // 8) * 128:1664 + (x // 8) * 128]
        shift = (128 - (x % 8) * 16) % 128
        fb[pl.ds(x, 72, stride=12), :] = pltpu.roll(tail, shift, 1) if shift else tail

    for cp in loads[6:]:
        cp.wait()
    for cp in halo:
        cp.wait_recv()

    fr = mm(moves_v[0:TOK, :], xc[...])
    xf = fr[:, 0:192]
    cot_f = fr[:, 192:384]
    cot = cot_f.astype(BF16)
    mean = jnp.sum(xf, axis=1, keepdims=True) * (1.0 / WIDTH)
    xm = xf - mean
    var = jnp.sum(xm * xm, axis=1, keepdims=True) * (1.0 / WIDTH)
    rdev = lax.rsqrt(var + 1e-05)
    xhat = xm * rdev
    normed = xhat.astype(BF16)
    wq, wk, wv = wqkv_v[:, 0:192], wqkv_v[:, 192:384], wqkv_v[:, 384:576]
    q = mm(normed, wq).astype(BF16)
    k = mm(normed, wk).astype(BF16)
    v = mm(normed, wv).astype(BF16)
    da = mm_nt(cot, wproj_v[...]).astype(BF16)

    id_all = jnp.concatenate([idb[i] for i in range(4)], axis=0).astype(BF16)
    id_row = mm(idt_v[:, 0:64], id_all) * idt_v[:, 128:256].astype(F32)
    id_cell = mm(id_row.astype(BF16), jnp.ones((128, 128), BF16))
    key = id_cell + idt_v[:, 256:384].astype(F32) * izl.astype(F32)
    classes = lax.broadcasted_iota(jnp.int32, (TOK, 128), 1).astype(F32)
    onehot = jnp.where(key == classes, 1.0, 0.0).astype(BF16)

    lane_head = lax.broadcasted_iota(jnp.int32, (WIN, WIDTH), 1) // 32
    scale = 32.0 ** (-0.5)
    atts, dqs, dks, dvs = [], [], [], []
    for w in range(2):
        rows = slice(w * WIN, (w + 1) * WIN)
        qw, kw, vw, daw = q[rows], k[rows], v[rows], da[rows]
        block = (mm_nt(onehot[rows], onehot[rows]) - 1.0) * 1e30
        att = dq = dk = dv = None
        for h in range(HEADS):
            here = lane_head == h
            zero = jnp.zeros((WIN, WIDTH), BF16)
            qh = jnp.where(here, qw, zero)
            kh = jnp.where(here, kw, zero)
            vh = jnp.where(here, vw, zero)
            dah = jnp.where(here, daw, zero)
            hr = slice(h * WIN, (h + 1) * WIN)
            bias = jnp.concatenate([fa[hr, :], fb[hr, 0:16]], axis=1)
            s = mm_nt(qh, kw) * scale + bias + block
            ex = jnp.exp(s - jnp.max(s, axis=1, keepdims=True))
            p = ex / jnp.sum(ex, axis=1, keepdims=True)
            pb = p.astype(BF16)
            dp = mm_nt(dah, vw)
            ds = p * (dp - jnp.sum(p * dp, axis=1, keepdims=True))
            dsb = ds.astype(BF16)
            ds_a = ds[:, 0:128]
            ds_b = jnp.concatenate([ds[:, 128:144], jnp.zeros((WIN, 112), F32)], axis=1)
            if w == 0:
                ba[hr, :] = ds_a
                bb[hr, :] = ds_b
            else:
                ba[hr, :] += ds_a
                bb[hr, :] += ds_b
            terms = (mm(pb, vh), mm(dsb, kh), mm_tn(dsb, qh), mm_tn(pb, dah))
            if h == 0:
                att, dq, dk, dv = terms
            else:
                att, dq, dk, dv = att + terms[0], dq + terms[1], dk + terms[2], dv + terms[3]
        atts.append(att.astype(BF16))
        dqs.append((dq * scale).astype(BF16))
        dks.append((dk * scale).astype(BF16))
        dvs.append(dv.astype(BF16))
    att = jnp.concatenate(atts, axis=0)
    dq = jnp.concatenate(dqs, axis=0)
    dk = jnp.concatenate(dks, axis=0)
    dv = jnp.concatenate(dvs, axis=0)

    gs[:, 0:192] = mm_tn(normed, dq)
    gs[:, 192:384] = mm_tn(normed, dk)
    gs[:, 384:576] = mm_tn(normed, dv)
    gs[:, 576:768] = mm_tn(att, cot)
    for i in range(ROWS_MAIN):
        for j in range(COLS_MAIN):
            pay[tile_place(i * COLS_MAIN + j)] = gs[
                i * 16:(i + 1) * 16, j * 128:(j + 1) * 128].astype(BF16)
    mains, tails = [], [None, None]
    for x in range(12):
        mains.append(ba[pl.ds(x, 72, stride=12), :])
        t = bb[pl.ds(x, 72, stride=12), :]
        if x % 8:
            t = pltpu.roll(t, (x % 8) * 16, 1)
        tails[x // 8] = t if tails[x // 8] is None else tails[x // 8] + t
    terms = jnp.concatenate(mains + tails, axis=1)
    t_hi = terms.astype(BF16)
    t_lo = (terms - t_hi.astype(F32)).astype(BF16)
    gb = mm_nt(t_hi, spread_v[...]) + mm_nt(t_lo, spread_v[...])
    gb = jnp.concatenate([gb, jnp.zeros((8, 384), F32)], axis=0)
    for which in range(2):
        mine = jnp.where(band == which, gb, 0.0).astype(BF16)
        for i in range(5):
            for j in range(3):
                pay[tile_place(72 + which * BIAS_TILES + i * 3 + j)] = mine[
                    i * 16:(i + 1) * 16, j * 128:(j + 1) * 128]
    for half in range(2):
        for t in range(HALF, CHUNKS * TILES):
            pay[half, t // TILES, t % TILES] = jnp.zeros((16, 128), BF16)

    order = [(group + d) % 8 for d in range(1, 9)]
    cores = [remote(pay.at[1 - core, j], rc.at[j], c_ss.at[d], c_rs.at[d], sibling)
             for d, j in enumerate(order)]
    for cp in cores:
        cp.start()

    dn = mm_nt(dq, wq) + mm_nt(dk, wk) + mm_nt(dv, wv)
    m1 = jnp.sum(dn, axis=1, keepdims=True) * (1.0 / WIDTH)
    m2 = jnp.sum(dn * xhat, axis=1, keepdims=True) * (1.0 / WIDTH)
    gf = (cot_f + rdev * (dn - m1 - xhat * m2)).astype(BF16)
    gback[0:TOK, :] = gf
    ret_b[...] = mm(cells_v[208:416, :], gf).astype(BF16)
    ret_to = [(lat, east), (lat_o, lon), (lat_o, east)]
    returns = [remote(ret_b.at[pl.ds(a, n)], gback.at[pl.ds(b, n)], r_ss.at[i], r_rs.at[i], ret_to[i])
               for i, (a, b, n, _) in enumerate(strips)]
    for cp in returns:
        cp.start()

    scatter = []
    for d, j in enumerate(order):
        cores[d].wait_recv()
        cur[j] = (pay[core, j].astype(F32) + rc[j].astype(F32)).astype(BF16)
        if d < 7:
            cp = remote(cur.at[j], ra.at[group], a_ss.at[d], a_rs.at[d], member(j))
            cp.start()
            scatter.append(cp)
    ra[group] = cur[group]

    for cp in returns:
        cp.wait_recv()
    field_ref[...] = mm(moves_v[TOK:2 * TOK, :], gback[...]).astype(BF16)

    def total(ref, n):
        acc = ref[0].astype(F32)
        for i in range(1, n):
            acc = acc + ref[i].astype(F32)
        return acc.astype(BF16)

    for cp in scatter:
        cp.wait_recv()
    ry[iy] = total(ra, 8)
    over_y = [remote(ry.at[iy], ry.at[iy], y_ss.at[d - 1], y_rs.at[d - 1], at_y((iy + d) % 8))
              for d in range(1, 8)]
    for cp in over_y:
        cp.start()
    for cp in over_y:
        cp.wait_recv()
    rz[izh] = total(ry, 8)
    over_z = [remote(rz.at[izh], rz.at[izh], z_ss.at[d - 1], z_rs.at[d - 1], at_zh((izh + d) % 4))
              for d in range(1, 4)]
    for cp in over_z:
        cp.start()
    for cp in over_z:
        cp.wait_recv()

    fin[core, group] = total(rz, 4)
    gather = [remote(fin.at[core, group], fin.at[core, group], g_ss.at[d - 1], g_rs.at[d - 1],
                     member((group + d) % 8)) for d in range(1, 8)]
    for cp in gather:
        cp.start()
    final = []
    for d in range(8):
        j = (group + 8 - d) % 8
        if d:
            gather[d - 1].wait_recv()
        cp = remote(fin.at[core, j], fin.at[core, j], k_ss.at[d], k_rs.at[d], sibling)
        cp.start()
        final.append(cp)
    for cp in final:
        cp.wait_recv()

    token_scale = 147456.0 ** (-0.5)
    for i in range(ROWS_MAIN):
        r = slice(i * 16, (i + 1) * 16)
        row = [fin[tile_place(i * COLS_MAIN + j)].astype(F32) * token_scale for j in range(COLS_MAIN)]
        for j in range(4):
            gqkv_ref[r, j * 128:(j + 1) * 128] = row[j]
        gqkv_ref[r, 512:576] = row[4][:, 0:64]
        gproj_ref[r, 0:64] = row[4][:, 64:128]
        gproj_ref[r, 64:192] = row[5]
    for which in range(2):
        for j in range(3):
            col = jnp.concatenate(
                [fin[tile_place(72 + which * BIAS_TILES + i * 3 + j)] for i in range(5)],
                axis=0).astype(F32)[0:72]
            for kk in range(4):
                part = pltpu.roll(col, 128 - 32 * kk, 1) if kk else col
                o2d[pl.ds(which * 1152 + 4 * j + kk, 72, stride=16), :] = part
        for h in range(HEADS):
            for a in range(12):
                r0 = which * 1152 + (h * 12 + a) * 16
                gbias_ref[which, h, a] = o2d[r0:r0 + 12, 0:23]

    for cp in halo + returns + cores + scatter + over_y + over_z + gather + final:
        cp.wait_send()


def body(grid_state, cotangent, mask_ids, earth_bias, qkv_weight, proj_weight):
    tables = [jnp.asarray(t) for t in build_tables()]
    vm = pltpu.VMEM
    dma = lambda n: pltpu.SemaphoreType.DMA((n,))
    scratch = [
        vm((TOK, WIDTH), BF16), vm((TOK, WIDTH), BF16), vm((2, 6, 24), jnp.int32),
        vm((6, 12, 12, 23), F32), vm((192, 576), BF16), vm((192, 192), BF16),
        vm((416, TOK), BF16), vm((576, ALL), BF16), vm((TOK, 384), BF16), vm((384, 1792), BF16),
        vm((ALL, 384), BF16), vm((208, 384), BF16), vm((4, 16, 128), F32), vm((1152, 128), F32),
        vm((864, 128), F32), vm((864, 128), F32), vm((864, 128), F32), vm((864, 128), F32),
        vm((ALL, WIDTH), BF16), vm((208, WIDTH), BF16), vm((192, 768), F32),
        vm((2, CHUNKS, TILES, 16, 128), BF16), vm((CHUNKS, TILES, 16, 128), BF16),
        vm((CHUNKS, TILES, 16, 128), BF16), vm((8, TILES, 16, 128), BF16),
        vm((8, TILES, 16, 128), BF16), vm((4, TILES, 16, 128), BF16),
        vm((2, CHUNKS, TILES, 16, 128), BF16), vm((2304, 128), F32),
        dma(10), dma(6), dma(6), dma(3), dma(3), dma(8), dma(8), dma(7), dma(7), dma(7), dma(7),
        dma(3), dma(3), dma(7), dma(7), dma(8), dma(8),
    ]
    any_space = pl.BlockSpec(memory_space=pl.ANY)
    in_vmem = pl.BlockSpec(memory_space=pltpu.VMEM)
    field, gqkv, gproj, gbias = pl.pallas_call(
        kernel,
        out_shape=(
            jax.ShapeDtypeStruct((TOK, WIDTH), BF16),
            jax.ShapeDtypeStruct((192, 576), F32),
            jax.ShapeDtypeStruct((192, 192), F32),
            jax.ShapeDtypeStruct((2, 6, 12, 12, 23), F32),
        ),
        in_specs=[any_space] * 10,
        out_specs=(in_vmem,) * 4,
        scratch_shapes=scratch,
        compiler_params=pltpu.CompilerParams(
            collective_id=0, has_side_effects=True, vmem_limit_bytes=48 * 2**20),
        name="window_backward",
    )(
        grid_state.reshape(TOK, WIDTH), cotangent.reshape(TOK, WIDTH), mask_ids, earth_bias,
        qkv_weight, proj_weight, *tables,
    )
    return field.reshape(grid_state.shape), gqkv, gproj, gbias


def solution(mesh):
    placed = (
        P(None, "lat", "lon", None),
        P(None, "lat", "lon", None),
        P(None, "lat", "lon"),
        P(),
        P(),
        P(),
    )
    return jax.shard_map(
        body,
        mesh=mesh,
        in_specs=placed,
        out_specs=(P(None, "lat", "lon", None), P(), P(), P()),
        check_vma=False,
    )
```

time: 404 us -> 63.9 us (0.16)
  waiting for transfers between devices: 267 us -> 0 us
  Pallas kernels: 0 us -> 57.1 us
  local copies, waits for them, and re-layouts: 56.8 us -> 5.86 us
  starting transfers between devices: 33 us -> 0 us
  matrix products: 19.8 us -> 0 us
  between operations: 14.6 us -> 0.76 us
  other arithmetic: 10.9 us -> 0 us
    psum x1 -> x0, waiting for transfers between devices: 263 us -> none  [body(): lax.psum((grad_qkv, grad_proj, placed), ('lat', 'lon'))]
    pallas_call x0 -> x1, Pallas kernels: none -> 57.1 us  [body(): pl.pallas_call(kernel, out_shape=(jax.ShapeDtypeStruct((TOK, WIDTH), BF16...]
    ppermute x8 -> x0, starting transfers between devices: 33 us -> none  [the longest x4 22.5 us: passed_along(): return lax.ppermute(block, axis, route)]
    dot_general x12 -> x0, matrix products: 17.7 us -> none  [the longest x1 5.97 us: window_grad(): jnp.einsum('rhaxby,xyo->rhabo', band_sum, offsets, precision=lax.Precisio...]
    add x2 -> x0, local copies, waits for them, and re-layouts: 17.4 us -> none  [window_grad(): scores = scores + full_bias[:, None]]
    another operation x9 -> x0, local copies, waits for them, and re-layouts: 12.9 us -> none
    dynamic_update_slice x1 -> x0, local copies, waits for them, and re-layouts: 9.31 us -> none  [body(): lax.dynamic_update_slice_in_dim(jnp.zeros(earth_bias.shape, jnp.float32),...]
    ppermute x8 -> x0, waiting for transfers between devices: 4.35 us -> none  [the longest x4 3.18 us: swapped(): lax.ppermute(array, axis, [(i, i ^ 1 << stride) for i in range(lax.axis_s...]
  transfers between devices with their start and end apart: 9 -> 0, of which waited for: 3 -> 0; matrix products, arithmetic and copies ran while one was open for 9% -> 0% of each run, Pallas kernels for 0% -> 0%
where the time goes in v1:
time: 63.9 us; the launch traced here: 63.7 us
  Pallas kernels  57.1 us (89%)
  local copies, waits for them, and re-layouts  5.86 us (9%)
  between operations  0.76 us (1%)
    pallas_call x1, Pallas kernels, body(): pl.pallas_call(kernel, out_shape=(jax.ShapeDtypeStruct((TOK, WIDTH), BF16...  57.1 us
    unnamed x20, local copies, waits for them, and re-layouts  5.86 us

profile of v1, /device:TPU:1, one launch (start us, length us, event | category | flops | bytes accessed | tf_op | source)
XLA Modules:
  0.0 63.7 jit_solution(465359373746821176)
XLA Ops:
  0.6 0.0 copy-start.3
  0.6 0.0 copy-start
  0.7 0.0 copy-start.1
  0.7 0.0 copy-start.6
  0.7 0.0 copy-start.2
  0.7 0.0 copy-start.5
  0.7 0.0 copy-start.4
  0.7 0.8 %copy.14.ids_hbm = s32[2,6,24]{2,1,0:T(8,128)S(1)} copy(s32[2,6,24]{2,0,1:T(2,128)} %param.12) | data formatting | bytes 2304 | tf_op args[2]
  1.5 1.3 %copy.15.eb_hbm = f32[2,6,12,12,23]{4,3,2,1,0:T(8,128)S(1)} copy(f32[2,6,12,12,23]{4,0,3,2,1:T(2,128)} %param.13) | data formatting | bytes 317952 | tf_op args[3]
  2.8 0.0 copy-done.3
  2.8 0.0 copy-done
  2.8 0.0 copy-done.1
  2.9 0.0 copy-done.6
  2.9 0.0 copy-done.2
  2.9 0.0 copy-done.5
  2.9 0.0 copy-done.4
  2.9 57.1 %window_backward.1 = (bf16[288,192]{1,0:T(8,128)(2,1)S(1)}, f32[192,576]{1,0:T(8,128)S(1)}, f32[192,192]{1,0:T(8,128)S(1)}, f32[2,6,12,12,23]{4,3,2,1,0:T(8,128)S(1)}) custom-call(bf16[288,192]{1,0:T(8,128)(2,1)S(1)} %bitcast.3, bf16[288,192]{1,0:T(8,128)(2,1)S(1)} %bitcast.4, s32[2,6,24]{2,1,0:T(8,128)S(1)} %copy.14.ids_hbm, ...), custom_call_target="tpu_custom_call" | custom-call | tf_op jit(solution)/shard_map/window_backward/pallas_call | solution.py:403
  60.0 1.6 %copy.16 = f32[2,6,12,12,23]{4,0,3,2,1:T(2,128)} copy(f32[2,6,12,12,23]{4,3,2,1,0:T(8,128)S(1)} %get-tuple-element.15) | data formatting | bytes 317952
  61.6 0.7 %copy.20 = bf16[2,6,24,192]{3,2,1,0:T(8,128)(2,1)} copy(bf16[2,6,24,192]{3,2,1,0:T(8,128)(2,1)S(1)} %bitcast.5) | data formatting | bytes 221184
  62.3 0.8 %copy.21 = f32[192,576]{1,0:T(8,128)} copy(f32[192,576]{1,0:T(8,128)S(1)} %get-tuple-element.21) | data formatting | bytes 884736
  63.0 0.7 %copy.22 = f32[192,192]{1,0:T(8,128)} copy(f32[192,192]{1,0:T(8,128)S(1)} %get-tuple-element.22) | data formatting | bytes 294912
Async XLA Ops:
  0.6 2.2 %copy-start.3 = (bf16[288,384]{1,0:T(8,128)(2,1)S(1)}, bf16[288,384]{1,0:T(8,128)(2,1)}, u32[]{:S(2)}) copy-start(bf16[288,384]{1,0:T(8,128)(2,1)} %constant.10.clone.idt_hbm) | copy-start | bytes 663556
  0.6 2.2 %copy-start = (bf16[576,496]{1,0:T(8,128)(2,1)S(1)}, bf16[576,496]{1,0:T(8,128)(2,1)}, u32[]{:S(2)}) copy-start(bf16[576,496]{1,0:T(8,128)(2,1)} %constant.9.clone.moves_hbm) | copy-start | bytes 1714180
  0.7 2.2 %copy-start.1 = (bf16[416,288]{1,0:T(8,128)(2,1)S(1)}, bf16[416,288]{1,0:T(8,128)(2,1)}, u32[]{:S(2)}) copy-start(bf16[416,288]{1,0:T(8,128)(2,1)} %constant.8.clone.cells_hbm) | copy-start | bytes 718852
  0.7 2.2 %copy-start.6 = (bf16[192,192]{1,0:T(8,128)(2,1)S(1)}, bf16[192,192]{1,0:T(8,128)(2,1)}, u32[]{:S(2)}) copy-start(bf16[192,192]{1,0:T(8,128)(2,1)} %wproj_hbm.1) | copy-start | bytes 221188
  0.7 2.2 %copy-start.2 = (bf16[192,576]{1,0:T(8,128)(2,1)S(1)}, bf16[192,576]{1,0:T(8,128)(2,1)}, u32[]{:S(2)}) copy-start(bf16[192,576]{1,0:T(8,128)(2,1)} %wqkv_hbm.1) | copy-start | bytes 663556
  0.7 2.2 %copy-start.5 = (bf16[2,6,24,192]{3,2,1,0:T(8,128)(2,1)S(1)}, bf16[2,6,24,192]{3,2,1,0:T(8,128)(2,1)}, u32[]{:S(2)}) copy-start(bf16[2,6,24,192]{3,2,1,0:T(8,128)(2,1)} %param.11) | copy-start | bytes 331780
  0.7 2.2 %copy-start.4 = (bf16[2,6,24,192]{3,2,1,0:T(8,128)(2,1)S(1)}, bf16[2,6,24,192]{3,2,1,0:T(8,128)(2,1)}, u32[]{:S(2)}) copy-start(bf16[2,6,24,192]{3,2,1,0:T(8,128)(2,1)} %param.10) | copy-start | bytes 331780

commit v2 on v1

v2 whole, which is shorter than its diff:
```python
import functools

import jax
import jax.numpy as jnp
import numpy as np
from jax import lax
from jax.experimental import pallas as pl
from jax.experimental.pallas import tpu as pltpu
from jax.sharding import PartitionSpec as P

MESH = pl.DeviceIdType.MESH
F32, BF16 = jnp.float32, jnp.bfloat16

TOK = 288
WIN = 144
WIDTH = 192
HEADS = 6
NEAR, FAR, EAST, CORNER, ALL = 288, 368, 416, 464, 512
STRIPS = ((0, NEAR, 80), (80, FAR, 48), (128, EAST, 48), (176, CORNER, 48))
SENT = 224
CHUNKS, TILES = 8, 7
MAIN, BIAS = 5, 2
HALF = 36
ROWS_MAIN, COLS_MAIN = 12, 6
BIAS_TILES = 15


def build_tables():
    natural = lambda z, r, c: (z * 6 + r) * 24 + c
    send = np.zeros((SENT, TOK), np.float32)
    for z in range(2):
        for r in range(3):
            row = z * 3 + r
            for c in range(12):
                send[row * 12 + c, natural(z, r, c + 6)] = 1
            for c in range(6):
                send[80 + row * 6 + c, natural(z, r, c + 18)] = 1
                send[128 + row * 6 + c, natural(z, r + 3, c)] = 1
                send[176 + row * 6 + c, natural(z, r, c)] = 1
    frame = np.zeros((TOK, ALL), np.float32)
    id_rows = np.zeros((TOK, 64), np.float32)
    id_cols = np.zeros((TOK, 128), np.float32)
    wrapped = np.zeros((TOK, 128), np.float32)
    for w in range(2):
        for z in range(2):
            for r in range(6):
                for p in range(12):
                    t = w * WIN + (z * 6 + r) * 12 + p
                    c = w * 12 + p
                    above = z * 3 + r - 3
                    if r < 3 and c < 18:
                        src, block, row, col = natural(z, r + 3, c + 6), 0, r + 3, c + 6
                    elif r < 3:
                        src, block, row, col = EAST + (z * 3 + r) * 6 + c - 18, 2, r + 3, c - 18
                    elif c < 12:
                        src, block, row, col = NEAR + above * 12 + c, 1, r - 3, c + 6
                    elif c < 18:
                        src, block, row, col = FAR + above * 6 + c - 12, 1, r - 3, c + 6
                    else:
                        src, block, row, col = CORNER + above * 6 + c - 18, 3, r - 3, c - 18
                    frame[t, src] = 1
                    id_rows[t, block * 16 + row * 2 + z] = 1
                    id_cols[t, col] = 1
                    wrapped[t, :] = 3.0 if r >= 3 else 0.0
    back = frame[:, TOK:].T
    out = np.concatenate([frame[:, :TOK].T, send.T], axis=1)
    spread = np.zeros((384, 1792), np.float32)
    for x in range(12):
        for b in range(12):
            for y in range(12):
                key = b * 12 + y
                col = x * 128 + key if key < 128 else 1536 + x * 16 + key - 128
                spread[b * 32 + x - y + 11, col] = 1
    cells = np.concatenate([send, back], axis=0)
    moves = np.concatenate([frame, out], axis=0)
    ids = np.concatenate([id_rows, np.zeros((TOK, 64), np.float32), id_cols, wrapped], axis=1)
    return [np.asarray(t, jnp.bfloat16) for t in (cells, moves, ids, spread)]


def mm(a, b):
    return lax.dot_general(a, b, (((1,), (0,)), ((), ())), preferred_element_type=F32)


def mm_nt(a, b):
    return lax.dot_general(a, b, (((1,), (1,)), ((), ())), preferred_element_type=F32)


def mm_tn(a, b):
    return lax.dot_general(a, b, (((0,), (0,)), ((), ())), preferred_element_type=F32)


def main_place(t):
    return t // HALF, (t % HALF) // MAIN, (t % HALF) % MAIN


def roll(a, shift):
    shift %= 128
    return pltpu.roll(a, shift, 1) if shift else a


def kernel(
    x_hbm, cot_hbm, ids_hbm, eb_hbm, wqkv_hbm, wproj_hbm, cells_hbm, moves_hbm, idt_hbm, spread_hbm,
    field_ref, fin,
    x_v, cot_v, ids_v, eb_v, wqkv_v, wproj_v, cells_v, moves_v, idt_v, spread_v,
    xc, send_b, idb, fa, fb, ba, bb, gback, ret_b, gs,
    pay_m, pay_b, rc_m, rc_b, cur, ra, ry, rz,
    in_sem, h_ss, h_rs, r_ss, r_rs, c_ss, c_rs, a_ss, a_rs, y_ss, y_rs, z_ss, z_rs,
    g_ss, g_rs, k_ss, k_rs,
):
    lat, lon = lax.axis_index("lat"), lax.axis_index("lon")
    iy, ix, izl = lat // 8, (lat // 2) % 4, lat % 2
    izh, core = lon // 2, lon % 2
    group = ix * 2 + izl
    band = izl

    lat_o = lat + 1 - 2 * izl
    east, west = (lon + 1) % 8, (lon + 7) % 8
    sibling = (lat, izh * 2 + 1 - core)

    def member(g):
        return (iy * 8 + g, lon)

    def at_y(y):
        return (y * 8 + group, lon)

    def at_zh(zh):
        return (lat, zh * 2 + core)

    barrier = pltpu.get_barrier_semaphore()
    partners = [(lat_o, lon), (lat, west), (lat, east), (lat_o, west), (lat_o, east), sibling]
    partners += [member((group + d) % 8) for d in range(1, 8)]
    partners += [at_y((iy + d) % 8) for d in range(1, 8)]
    partners += [at_zh((izh + d) % 4) for d in range(1, 4)]
    for p in partners:
        pl.semaphore_signal(barrier, inc=1, device_id=p, device_id_type=MESH)

    srcs = [x_hbm, cot_hbm, cells_hbm, ids_hbm, eb_hbm, spread_hbm, moves_hbm, idt_hbm,
            wqkv_hbm, wproj_hbm]
    dsts = [x_v, cot_v, cells_v, ids_v, eb_v, spread_v, moves_v, idt_v, wqkv_v, wproj_v]
    loads = [pltpu.make_async_copy(s, d, in_sem.at[i]) for i, (s, d) in enumerate(zip(srcs, dsts))]
    for cp in loads:
        cp.start()

    loads[0].wait()
    loads[1].wait()
    loads[2].wait()
    loads[3].wait()
    xc[0:TOK, 0:192] = x_v[...]
    xc[0:TOK, 192:384] = cot_v[...]
    send_b[...] = mm(cells_v[0:SENT, :], xc[0:TOK, :]).astype(BF16)
    idb[0] = jnp.zeros((16, 128), F32)
    idb[0, 0:12, 0:24] = ids_v.reshape(12, 24)[...].astype(F32)

    pl.semaphore_wait(barrier, len(partners))

    def remote(src, dst, ss, rs, dev):
        return pltpu.make_async_remote_copy(
            src_ref=src, dst_ref=dst, send_sem=ss, recv_sem=rs, device_id=dev, device_id_type=MESH)

    strip_to = [(lat_o, lon), (lat_o, lon), (lat, west), (lat_o, west)]
    id_to = [(lat_o, lon), (lat, west), (lat_o, west)]
    strips = [remote(send_b.at[pl.ds(a, n)], xc.at[pl.ds(b, n)], h_ss.at[i], h_rs.at[i], strip_to[i])
              for i, (a, b, n) in enumerate(STRIPS)]
    id_blocks = [remote(idb.at[0], idb.at[i + 1], h_ss.at[4 + i], h_rs.at[4 + i], id_to[i])
                 for i in range(3)]
    halo = [id_blocks[0], strips[0], id_blocks[1], strips[2], id_blocks[2], strips[3], strips[1]]
    for cp in halo:
        cp.start()

    loads[4].wait()
    loads[5].wait()
    eb_rows = eb_v.reshape(1728, 23)
    nothing = jnp.zeros((72, 105), F32)
    packs = []
    for g in range(3):
        acc = None
        for k in range(4):
            part = eb_rows[pl.ds(2 * (4 * g + k) + band, 72, stride=24), :]
            part = roll(jnp.concatenate([part, nothing], axis=1), 32 * k)
            acc = part if acc is None else acc + part
        packs.append(acc)
    e = jnp.concatenate(packs, axis=1)
    hi = e.astype(BF16)
    rest = e - hi.astype(F32)
    mid = rest.astype(BF16)
    low = (rest - mid.astype(F32)).astype(BF16)
    full = (mm(hi, spread_v[...]) + mm(mid, spread_v[...])) + mm(low, spread_v[...])
    for x in range(12):
        fa[pl.ds(x, 72, stride=12), :] = full[:, x * 128:(x + 1) * 128]
        tail = full[:, 1536 + (x // 8) * 128:1664 + (x // 8) * 128]
        fb[pl.ds(x, 72, stride=12), :] = roll(tail, -16 * x)

    for cp in loads[6:]:
        cp.wait()
    wq, wk, wv = wqkv_v[:, 0:192], wqkv_v[:, 192:384], wqkv_v[:, 384:576]
    lane_head = lax.broadcasted_iota(jnp.int32, (WIN, WIDTH), 1) // 32
    classes = lax.broadcasted_iota(jnp.int32, (WIN, 128), 1).astype(F32)
    ones = jnp.ones((128, 128), BF16)
    scale = 32.0 ** (-0.5)

    kept = []
    for w in range(2):
        rows = slice(w * WIN, (w + 1) * WIN)
        if w == 0:
            id_blocks[0].wait_recv()
            strips[0].wait_recv()
        else:
            for cp in halo[2:]:
                cp.wait_recv()
        width, blocks = (FAR, 2) if w == 0 else (ALL, 4)
        fr = mm(moves_v[rows, 0:width], xc[0:width, :])
        xf = fr[:, 0:192]
        cot_f = fr[:, 192:384]
        cot = cot_f.astype(BF16)
        mean = jnp.sum(xf, axis=1, keepdims=True) * (1.0 / WIDTH)
        xm = xf - mean
        var = jnp.sum(xm * xm, axis=1, keepdims=True) * (1.0 / WIDTH)
        rdev = lax.rsqrt(var + 1e-05)
        xhat = xm * rdev
        normed = xhat.astype(BF16)
        qw = mm(normed, wq).astype(BF16)
        kw = mm(normed, wk).astype(BF16)
        vw = mm(normed, wv).astype(BF16)
        daw = mm_nt(cot, wproj_v[...]).astype(BF16)

        id_all = jnp.concatenate([idb[i] for i in range(blocks)], axis=0).astype(BF16)
        id_row = mm(idt_v[rows, 0:16 * blocks], id_all) * idt_v[rows, 128:256].astype(F32)
        id_cell = mm(id_row.astype(BF16), ones)
        key = id_cell + idt_v[rows, 256:384].astype(F32) * izl.astype(F32)
        onehot = jnp.where(key == classes, 1.0, 0.0).astype(BF16)
        block = (mm_nt(onehot, onehot) - 1.0) * 1e30

        att = dq = dk = dv = None
        for h in range(HEADS):
            here = lane_head == h
            zero = jnp.zeros((WIN, WIDTH), BF16)
            qh = jnp.where(here, qw, zero)
            kh = jnp.where(here, kw, zero)
            vh = jnp.where(here, vw, zero)
            dah = jnp.where(here, daw, zero)
            hr = slice(h * WIN, (h + 1) * WIN)
            bias = jnp.concatenate([fa[hr, :], fb[hr, 0:16]], axis=1)
            s = mm_nt(qh, kw) * scale + bias + block
            ex = jnp.exp(s - jnp.max(s, axis=1, keepdims=True))
            p = ex * (1.0 / jnp.sum(ex, axis=1, keepdims=True))
            pb = p.astype(BF16)
            dp = mm_nt(dah, vw)
            ds = p * (dp - jnp.sum(p * dp, axis=1, keepdims=True))
            dsb = ds.astype(BF16)
            ds_a = ds[:, 0:128]
            ds_b = jnp.concatenate([ds[:, 128:144], jnp.zeros((WIN, 112), F32)], axis=1)
            if w == 0:
                ba[hr, :] = ds_a
                bb[hr, :] = ds_b
            else:
                ba[hr, :] += ds_a
                bb[hr, :] += ds_b
            terms = (mm(pb, vh), mm(dsb, kh), mm_tn(dsb, qh), mm_tn(pb, dah))
            if h == 0:
                att, dq, dk, dv = terms
            else:
                att, dq, dk, dv = att + terms[0], dq + terms[1], dk + terms[2], dv + terms[3]
        kept.append((normed, cot, att.astype(BF16), (dq * scale).astype(BF16),
                     (dk * scale).astype(BF16), dv.astype(BF16), cot_f, xhat, rdev))
    normed, cot, att, dq, dk, dv, cot_f, xhat, rdev = [
        jnp.concatenate(pair, axis=0) for pair in zip(*kept)]

    gs[:, 0:192] = mm_tn(normed, dq)
    gs[:, 192:384] = mm_tn(normed, dk)
    gs[:, 384:576] = mm_tn(normed, dv)
    gs[:, 576:768] = mm_tn(att, cot)
    for i in range(ROWS_MAIN):
        for j in range(COLS_MAIN):
            pay_m[main_place(i * COLS_MAIN + j)] = gs[
                i * 16:(i + 1) * 16, j * 128:(j + 1) * 128].astype(BF16)
    for half in range(2):
        for t in range(HALF, CHUNKS * MAIN):
            pay_m[half, t // MAIN, t % MAIN] = jnp.zeros((16, 128), BF16)
    cores = [remote(pay_m.at[1 - core], rc_m, c_ss.at[0], c_rs.at[0], sibling)]
    cores[0].start()

    mains, tails = [], [None, None]
    for x in range(12):
        mains.append(ba[pl.ds(x, 72, stride=12), :])
        t = roll(bb[pl.ds(x, 72, stride=12), :], 16 * x)
        tails[x // 8] = t if tails[x // 8] is None else tails[x // 8] + t
    terms = jnp.concatenate(mains + tails, axis=1)
    t_hi = terms.astype(BF16)
    t_lo = (terms - t_hi.astype(F32)).astype(BF16)
    gb = mm_nt(t_hi, spread_v[...]) + mm_nt(t_lo, spread_v[...])
    gb = jnp.concatenate([gb, jnp.zeros((8, 384), F32)], axis=0)
    for which in range(2):
        mine = jnp.where(band == which, gb, 0.0).astype(BF16)
        for t in range(BIAS_TILES):
            i, j = t // 3, t % 3
            pay_b[which, t // BIAS, t % BIAS] = mine[i * 16:(i + 1) * 16, j * 128:(j + 1) * 128]
        pay_b[which, CHUNKS - 1, BIAS - 1] = jnp.zeros((16, 128), BF16)
    cores.append(remote(pay_b.at[1 - core], rc_b, c_ss.at[1], c_rs.at[1], sibling))
    cores[1].start()

    for cp in cores:
        cp.wait_recv()
    order = [(group + d) % 8 for d in range(1, 8)]
    scatter = []
    for d, j in enumerate(order + [group]):
        cur[j, 0:MAIN] = (pay_m[core, j].astype(F32) + rc_m[j].astype(F32)).astype(BF16)
        cur[j, MAIN:TILES] = (pay_b[core, j].astype(F32) + rc_b[j].astype(F32)).astype(BF16)
        if d < 7:
            cp = remote(cur.at[j], ra.at[group], a_ss.at[d], a_rs.at[d], member(j))
            cp.start()
            scatter.append(cp)
    ra[group] = cur[group]

    dn = mm_nt(dq, wq) + mm_nt(dk, wk) + mm_nt(dv, wv)
    m1 = jnp.sum(dn, axis=1, keepdims=True) * (1.0 / WIDTH)
    m2 = jnp.sum(dn * xhat, axis=1, keepdims=True) * (1.0 / WIDTH)
    gf = (cot_f + rdev * (dn - m1 - xhat * m2)).astype(BF16)
    gback[0:TOK, :] = gf
    ret_b[...] = mm(cells_v[SENT:2 * SENT, :], gf).astype(BF16)
    ret_to = [(lat_o, lon), (lat_o, lon), (lat, east), (lat_o, east)]
    returns = [remote(ret_b.at[pl.ds(a, n)], gback.at[pl.ds(b, n)], r_ss.at[i], r_rs.at[i], ret_to[i])
               for i, (a, b, n) in enumerate(STRIPS)]
    for cp in returns:
        cp.start()

    def total(ref, n):
        acc = ref[0].astype(F32)
        for i in range(1, n):
            acc = acc + ref[i].astype(F32)
        return acc.astype(BF16)

    for cp in scatter:
        cp.wait_recv()
    ry[iy] = total(ra, 8)
    over_y = [remote(ry.at[iy], ry.at[iy], y_ss.at[d - 1], y_rs.at[d - 1], at_y((iy + d) % 8))
              for d in range(1, 8)]
    for cp in over_y:
        cp.start()

    for cp in returns:
        cp.wait_recv()
    field_ref[...] = mm(moves_v[TOK:2 * TOK, :], gback[...]).astype(BF16)

    for cp in over_y:
        cp.wait_recv()
    rz[izh] = total(ry, 8)
    over_z = [remote(rz.at[izh], rz.at[izh], z_ss.at[d - 1], z_rs.at[d - 1], at_zh((izh + d) % 4))
              for d in range(1, 4)]
    for cp in over_z:
        cp.start()
    for cp in over_z:
        cp.wait_recv()

    fin[core, group] = total(rz, 4)
    gather = [remote(fin.at[core, group], fin.at[core, group], g_ss.at[d - 1], g_rs.at[d - 1],
                     member((group + d) % 8)) for d in range(1, 8)]
    for cp in gather:
        cp.start()
    final = []
    for d in range(8):
        j = (group + 8 - d) % 8
        if d:
            gather[d - 1].wait_recv()
        cp = remote(fin.at[core, j], fin.at[core, j], k_ss.at[d], k_rs.at[d], sibling)
        cp.start()
        final.append(cp)
    for cp in final:
        cp.wait_recv()
    for cp in halo + returns + cores + scatter + over_y + over_z + gather + final:
        cp.wait_send()


def unpack(field_in, fin, field_ref, gqkv_ref, gproj_ref, gbias_ref):
    field_ref[...] = field_in[...]
    token_scale = 147456.0 ** (-0.5)
    for i in range(ROWS_MAIN):
        r = slice(i * 16, (i + 1) * 16)
        row = [fin[main_place(i * COLS_MAIN + j)].astype(F32) * token_scale for j in range(COLS_MAIN)]
        for j in range(4):
            gqkv_ref[r, j * 128:(j + 1) * 128] = row[j]
        gqkv_ref[r, 512:576] = row[4][:, 0:64]
        gproj_ref[r, 0:64] = row[4][:, 64:128]
        gproj_ref[r, 64:192] = row[5]
    bias_rows = gbias_ref.reshape(1728, 23)
    for which in range(2):
        for j in range(3):
            places = [i * 3 + j for i in range(5)]
            col = jnp.concatenate(
                [fin[which, t // BIAS, MAIN + t % BIAS] for t in places], axis=0).astype(F32)[0:72]
            for k in range(4):
                bias_rows[pl.ds(2 * (4 * j + k) + which, 72, stride=24), :] = roll(col, -32 * k)[:, 0:23]


def body(grid_state, cotangent, mask_ids, earth_bias, qkv_weight, proj_weight):
    tables = [jnp.asarray(t) for t in build_tables()]
    vm = pltpu.VMEM
    dma = lambda n: pltpu.SemaphoreType.DMA((n,))
    tiles = lambda *n: vm((*n, 16, 128), BF16)
    scratch = [
        vm((TOK, WIDTH), BF16), vm((TOK, WIDTH), BF16), vm((6, 2, 24), jnp.int32),
        vm((864, 2, 23), F32), vm((192, 576), BF16), vm((192, 192), BF16),
        vm((2 * SENT, TOK), BF16), vm((2 * TOK, ALL), BF16), vm((TOK, 384), BF16),
        vm((384, 1792), BF16),
        vm((ALL, 384), BF16), vm((SENT, 384), BF16), vm((4, 16, 128), F32),
        vm((864, 128), F32), vm((864, 128), F32), vm((864, 128), F32), vm((864, 128), F32),
        vm((ALL, WIDTH), BF16), vm((SENT, WIDTH), BF16), vm((192, 768), F32),
        tiles(2, CHUNKS, MAIN), tiles(2, CHUNKS, BIAS), tiles(CHUNKS, MAIN), tiles(CHUNKS, BIAS),
        tiles(CHUNKS, TILES), tiles(8, TILES), tiles(8, TILES), tiles(4, TILES),
        dma(10), dma(7), dma(7), dma(4), dma(4), dma(2), dma(2), dma(7), dma(7), dma(7), dma(7),
        dma(3), dma(3), dma(7), dma(7), dma(8), dma(8),
    ]
    any_space = pl.BlockSpec(memory_space=pl.ANY)
    in_vmem = pl.BlockSpec(memory_space=pltpu.VMEM)
    field, fin = pl.pallas_call(
        kernel,
        out_shape=(
            jax.ShapeDtypeStruct((TOK, WIDTH), BF16),
            jax.ShapeDtypeStruct((2, CHUNKS, TILES, 16, 128), BF16),
        ),
        in_specs=[any_space] * 10,
        out_specs=(in_vmem,) * 2,
        scratch_shapes=scratch,
        compiler_params=pltpu.CompilerParams(
            collective_id=0, has_side_effects=True, vmem_limit_bytes=48 * 2**20),
        name="window_backward",
    )(
        *[pltpu.with_memory_space_constraint(o, pltpu.HBM) for o in (grid_state.reshape(TOK, WIDTH), cotangent.reshape(TOK, WIDTH),
        mask_ids.transpose(1, 0, 2), earth_bias.transpose(1, 2, 3, 0, 4).reshape(864, 2, 23),
        qkv_weight, proj_weight, *tables)]
    )
    field, gqkv, gproj, gbias = pl.pallas_call(
        unpack,
        out_shape=(
            jax.ShapeDtypeStruct((TOK, WIDTH), BF16),
            jax.ShapeDtypeStruct((192, 576), F32),
            jax.ShapeDtypeStruct((192, 192), F32),
            jax.ShapeDtypeStruct((864, 2, 23), F32),
        ),
        in_specs=[in_vmem] * 2,
        out_specs=(in_vmem,) * 4,
        compiler_params=pltpu.CompilerParams(vmem_limit_bytes=16 * 2**20),
        name="unpack",
    )(field, fin)
    gbias = gbias.reshape(6, 12, 12, 2, 23).transpose(3, 0, 1, 2, 4)
    return field.reshape(grid_state.shape), gqkv, gproj, gbias


def solution(mesh):
    placed = (
        P(None, "lat", "lon", None),
        P(None, "lat", "lon", None),
        P(None, "lat", "lon"),
        P(),
        P(),
        P(),
    )
    return jax.shard_map(
        body,
        mesh=mesh,
        in_specs=placed,
        out_specs=(P(None, "lat", "lon", None), P(), P(), P()),
        check_vma=False,
    )
```

time: 63.9 us -> 57.9 us (0.906)
  local copies, waits for them, and re-layouts: 5.86 us -> 0 us
    unnamed x20 -> x0, local copies, waits for them, and re-layouts: 5.86 us -> none
    pallas_call x0 -> x1, Pallas kernels: none -> 1.46 us  [body(): pl.pallas_call(unpack, out_shape=(jax.ShapeDtypeStruct((TOK, WIDTH), BF16...]
    pallas_call x1, Pallas kernels: 57.1 us -> 55.6 us  [body(): pl.pallas_call(kernel, out_shape=(jax.ShapeDtypeStruct((TOK, WIDTH), BF16...]
where the time goes in v2:
time: 57.9 us; the launch traced here: 57.7 us
  Pallas kernels  57.1 us (99%)
  between operations  0.64 us (1%)
    pallas_call x1, Pallas kernels, body(): pl.pallas_call(kernel, out_shape=(jax.ShapeDtypeStruct((TOK, WIDTH), BF16...  55.6 us
    pallas_call x1, Pallas kernels, body(): pl.pallas_call(unpack, out_shape=(jax.ShapeDtypeStruct((TOK, WIDTH), BF16...  1.46 us

profile of v2, /device:TPU:1, one launch (start us, length us, event | category | flops | bytes accessed | tf_op | source)
XLA Modules:
  0.0 57.7 jit_solution(4985704708601081827)
XLA Ops:
  0.6 55.6 %window_backward.1 = (bf16[288,192]{1,0:T(8,128)(2,1)S(1)}, bf16[2,8,7,16,128]{4,3,2,1,0:T(8,128)(2,1)S(1)}) custom-call(bf16[288,192]{1,0:T(8,128)(2,1)} %bitcast.11, bf16[288,192]{1,0:T(8,128)(2,1)} %bitcast.12, s32[6,2,24]{2,1,0:T(2,128)} %bitcast.13, f32[864,2,23]{2,1,0:T(2,128)} %bitcast.10, bf16[192,576]{1,0:T(8,128)(2,1)} %wqkv_hbm.1, ...), custom_call_target="tpu_custom_call" | custom-call | tf_op jit(solution)/shard_map/window_backward/pallas_call | solution.py:414
  56.3 1.5 %unpack.1 = (bf16[288,192]{1,0:T(8,128)(2,1)}, f32[192,576]{1,0:T(8,128)}, f32[192,192]{1,0:T(8,128)}, f32[864,2,23]{2,1,0:T(2,128)}) custom-call(bf16[288,192]{1,0:T(8,128)(2,1)S(1)} %get-tuple-element.10.field_in, bf16[2,8,7,16,128]{4,3,2,1,0:T(8,128)(2,1)S(1)} %get-tuple-element.11.fin), custom_call_target="tpu_custom_call" | custom-call | tf_op jit(solution)/shard_map/unpack/pallas_call | solution.py:431

commit v3 on v2

--- a/solution.py
+++ b/solution.py
@@ -110,27 +110,44 @@
     lat, lon = lax.axis_index("lat"), lax.axis_index("lon")
     iy, ix, izl = lat // 8, (lat // 2) % 4, lat % 2
     izh, core = lon // 2, lon % 2
-    group = ix * 2 + izl
+    iz = izh * 2 + izl
     band = izl
 
     lat_o = lat + 1 - 2 * izl
     east, west = (lon + 1) % 8, (lon + 7) % 8
     sibling = (lat, izh * 2 + 1 - core)
 
+    def pick(a, b):
+        return a * (1 - core) + b * core
+
     def member(g):
-        return (iy * 8 + g, lon)
-
-    def at_y(y):
-        return (y * 8 + group, lon)
-
-    def at_zh(zh):
-        return (lat, zh * 2 + core)
+        return (pick(iy * 8 + g, g * 8 + ix * 2 + izl), lon)
+
+    def second(i):
+        return (pick(i * 8 + ix * 2 + izl, iy * 8 + ix * 2 + i % 2), pick(lon, (i // 2) * 2 + core))
+
+    def third(i):
+        return (pick(lat, iy * 8 + i * 2 + izl), pick(i * 2 + core, lon))
+
+    group, place2, place3 = pick(ix * 2 + izl, iy), pick(iy, iz), pick(izh, ix)
+    far8, far4 = (4, 3, 5, 2, 6, 1, 7), (2, 1, 3)
+    turns = ((2, 1), (1, 1), (3, 1), (2, 0), (1, 0), (3, 0), (0, 1))
+
+    def first_to(i, way):
+        dx, dz = turns[i]
+        to_x, to_z = (ix + way * dx + 4) % 4, (izl + dz) % 2
+        return pick(to_x * 2 + to_z, (iy + way * far8[i] + 8) % 8)
+
+    to_first = [first_to(i, 1) for i in range(7)]
+    from_first = [first_to(i, -1) for i in range(7)]
+    to_second = [(place2 + d) % 8 for d in far8]
+    to_third = [(place3 + d) % 4 for d in far4]
 
     barrier = pltpu.get_barrier_semaphore()
     partners = [(lat_o, lon), (lat, west), (lat, east), (lat_o, west), (lat_o, east), sibling]
-    partners += [member((group + d) % 8) for d in range(1, 8)]
-    partners += [at_y((iy + d) % 8) for d in range(1, 8)]
-    partners += [at_zh((izh + d) % 4) for d in range(1, 4)]
+    partners += [member(j) for j in to_first]
+    partners += [second(j) for j in to_second]
+    partners += [third(j) for j in to_third]
     for p in partners:
         pl.semaphore_signal(barrier, inc=1, device_id=p, device_id_type=MESH)
 
@@ -300,9 +317,8 @@
 
     for cp in cores:
         cp.wait_recv()
-    order = [(group + d) % 8 for d in range(1, 8)]
     scatter = []
-    for d, j in enumerate(order + [group]):
+    for d, j in enumerate(to_first + [group]):
         cur[j, 0:MAIN] = (pay_m[core, j].astype(F32) + rc_m[j].astype(F32)).astype(BF16)
         cur[j, MAIN:TILES] = (pay_b[core, j].astype(F32) + rc_b[j].astype(F32)).astype(BF16)
         if d < 7:
@@ -331,9 +347,9 @@
 
     for cp in scatter:
         cp.wait_recv()
-    ry[iy] = total(ra, 8)
-    over_y = [remote(ry.at[iy], ry.at[iy], y_ss.at[d - 1], y_rs.at[d - 1], at_y((iy + d) % 8))
-              for d in range(1, 8)]
+    ry[place2] = total(ra, 8)
+    over_y = [remote(ry.at[place2], ry.at[place2], y_ss.at[i], y_rs.at[i], second(j))
+              for i, j in enumerate(to_second)]
     for cp in over_y:
         cp.start()
 
@@ -343,25 +359,25 @@
 
     for cp in over_y:
         cp.wait_recv()
-    rz[izh] = total(ry, 8)
-    over_z = [remote(rz.at[izh], rz.at[izh], z_ss.at[d - 1], z_rs.at[d - 1], at_zh((izh + d) % 4))
-              for d in range(1, 4)]
+    rz[place3] = total(ry, 8)
+    over_z = [remote(rz.at[place3], rz.at[place3], z_ss.at[i], z_rs.at[i], third(j))
+              for i, j in enumerate(to_third)]
     for cp in over_z:
         cp.start()
     for cp in over_z:
         cp.wait_recv()
 
     fin[core, group] = total(rz, 4)
-    gather = [remote(fin.at[core, group], fin.at[core, group], g_ss.at[d - 1], g_rs.at[d - 1],
-                     member((group + d) % 8)) for d in range(1, 8)]
+    gather = [remote(fin.at[core, group], fin.at[core, group], g_ss.at[i], g_rs.at[i], member(j))
+              for i, j in enumerate(to_first)]
     for cp in gather:
         cp.start()
     final = []
-    for d in range(8):
-        j = (group + 8 - d) % 8
-        if d:
-            gather[d - 1].wait_recv()
-        cp = remote(fin.at[core, j], fin.at[core, j], k_ss.at[d], k_rs.at[d], sibling)
+    for i in (7, 6, 5, 4, 3, 2, 1, 0):
+        if i < 7:
+            gather[i].wait_recv()
+        j = group if i == 7 else from_first[i]
+        cp = remote(fin.at[core, j], fin.at[core, j], k_ss.at[i], k_rs.at[i], sibling)
         cp.start()
         final.append(cp)
     for cp in final:

time: 57.9 us -> 52.8 us (0.912)
  Pallas kernels: 57.1 us -> 52 us
    pallas_call x1, Pallas kernels: 55.6 us -> 50.6 us  [body(): pl.pallas_call(kernel, out_shape=(jax.ShapeDtypeStruct((TOK, WIDTH), BF16...]
where the time goes in v3:
time: 52.8 us; the launch traced here: 52.7 us
  Pallas kernels  52 us (98%)
  between operations  0.64 us (1%)
    pallas_call x1, Pallas kernels, body(): pl.pallas_call(kernel, out_shape=(jax.ShapeDtypeStruct((TOK, WIDTH), BF16...  50.6 us
    pallas_call x1, Pallas kernels, body(): pl.pallas_call(unpack, out_shape=(jax.ShapeDtypeStruct((TOK, WIDTH), BF16...  1.46 us

profile of v3, /device:TPU:1, one launch (start us, length us, event | category | flops | bytes accessed | tf_op | source)
XLA Modules:
  0.0 52.7 jit_solution(6861827561272755110)
XLA Ops:
  0.6 50.6 %window_backward.1 = (bf16[288,192]{1,0:T(8,128)(2,1)S(1)}, bf16[2,8,7,16,128]{4,3,2,1,0:T(8,128)(2,1)S(1)}) custom-call(bf16[288,192]{1,0:T(8,128)(2,1)} %bitcast.11, bf16[288,192]{1,0:T(8,128)(2,1)} %bitcast.12, s32[6,2,24]{2,1,0:T(2,128)} %bitcast.13, f32[864,2,23]{2,1,0:T(2,128)} %bitcast.10, bf16[192,576]{1,0:T(8,128)(2,1)} %wqkv_hbm.1, ...), custom_call_target="tpu_custom_call" | custom-call | tf_op jit(solution)/shard_map/window_backward/pallas_call | solution.py:430
  51.2 1.5 %unpack.1 = (bf16[288,192]{1,0:T(8,128)(2,1)}, f32[192,576]{1,0:T(8,128)}, f32[192,192]{1,0:T(8,128)}, f32[864,2,23]{2,1,0:T(2,128)}) custom-call(bf16[288,192]{1,0:T(8,128)(2,1)S(1)} %get-tuple-element.10.field_in, bf16[2,8,7,16,128]{4,3,2,1,0:T(8,128)(2,1)S(1)} %get-tuple-element.11.fin), custom_call_target="tpu_custom_call" | custom-call | tf_op jit(solution)/shard_map/unpack/pallas_call | solution.py:447

commit v4 on v3

--- a/solution.py
+++ b/solution.py
@@ -15,9 +15,10 @@
 WIN = 144
 WIDTH = 192
 HEADS = 6
-NEAR, FAR, EAST, CORNER, ALL = 288, 368, 416, 464, 512
-STRIPS = ((0, NEAR, 80), (80, FAR, 48), (128, EAST, 48), (176, CORNER, 48))
-SENT = 224
+SWAP, EAST, CORNER, ALL = 288, 400, 448, 496
+STRIPS = ((0, SWAP, 112), (112, EAST, 48), (160, CORNER, 48))
+SENT = 208
+STACK = 6
 CHUNKS, TILES = 8, 7
 MAIN, BIAS = 5, 2
 HALF = 36
@@ -31,12 +32,11 @@
     for z in range(2):
         for r in range(3):
             row = z * 3 + r
-            for c in range(12):
-                send[row * 12 + c, natural(z, r, c + 6)] = 1
+            for c in range(18):
+                send[row * 18 + c, natural(z, r, c + 6)] = 1
             for c in range(6):
-                send[80 + row * 6 + c, natural(z, r, c + 18)] = 1
-                send[128 + row * 6 + c, natural(z, r + 3, c)] = 1
-                send[176 + row * 6 + c, natural(z, r, c)] = 1
+                send[112 + row * 6 + c, natural(z, r + 3, c)] = 1
+                send[160 + row * 6 + c, natural(z, r, c)] = 1
     frame = np.zeros((TOK, ALL), np.float32)
     id_rows = np.zeros((TOK, 64), np.float32)
     id_cols = np.zeros((TOK, 128), np.float32)
@@ -52,10 +52,8 @@
                         src, block, row, col = natural(z, r + 3, c + 6), 0, r + 3, c + 6
                     elif r < 3:
                         src, block, row, col = EAST + (z * 3 + r) * 6 + c - 18, 2, r + 3, c - 18
-                    elif c < 12:
-                        src, block, row, col = NEAR + above * 12 + c, 1, r - 3, c + 6
                     elif c < 18:
-                        src, block, row, col = FAR + above * 6 + c - 12, 1, r - 3, c + 6
+                        src, block, row, col = SWAP + above * 18 + c, 1, r - 3, c + 6
                     else:
                         src, block, row, col = CORNER + above * 6 + c - 18, 3, r - 3, c - 18
                     frame[t, src] = 1
@@ -102,7 +100,7 @@
     x_hbm, cot_hbm, ids_hbm, eb_hbm, wqkv_hbm, wproj_hbm, cells_hbm, moves_hbm, idt_hbm, spread_hbm,
     field_ref, fin,
     x_v, cot_v, ids_v, eb_v, wqkv_v, wproj_v, cells_v, moves_v, idt_v, spread_v,
-    xc, send_b, idb, fa, fb, ba, bb, gback, ret_b, gs,
+    xc, send_b, idb, fa, fb, ba, bb, gback, ret_b, dqkv,
     pay_m, pay_b, rc_m, rc_b, cur, ra, ry, rz,
     in_sem, h_ss, h_rs, r_ss, r_rs, c_ss, c_rs, a_ss, a_rs, y_ss, y_rs, z_ss, z_rs,
     g_ss, g_rs, k_ss, k_rs,
@@ -143,6 +141,13 @@
     to_second = [(place2 + d) % 8 for d in far8]
     to_third = [(place3 + d) % 4 for d in far4]
 
+    srcs = [x_hbm, cot_hbm, cells_hbm, ids_hbm, eb_hbm, spread_hbm, moves_hbm, idt_hbm,
+            wqkv_hbm, wproj_hbm]
+    dsts = [x_v, cot_v, cells_v, ids_v, eb_v, spread_v, moves_v, idt_v, wqkv_v, wproj_v]
+    loads = [pltpu.make_async_copy(s, d, in_sem.at[i]) for i, (s, d) in enumerate(zip(srcs, dsts))]
+    for cp in loads[:4]:
+        cp.start()
+
     barrier = pltpu.get_barrier_semaphore()
     partners = [(lat_o, lon), (lat, west), (lat, east), (lat_o, west), (lat_o, east), sibling]
     partners += [member(j) for j in to_first]
@@ -150,23 +155,19 @@
     partners += [third(j) for j in to_third]
     for p in partners:
         pl.semaphore_signal(barrier, inc=1, device_id=p, device_id_type=MESH)
-
-    srcs = [x_hbm, cot_hbm, cells_hbm, ids_hbm, eb_hbm, spread_hbm, moves_hbm, idt_hbm,
-            wqkv_hbm, wproj_hbm]
-    dsts = [x_v, cot_v, cells_v, ids_v, eb_v, spread_v, moves_v, idt_v, wqkv_v, wproj_v]
-    loads = [pltpu.make_async_copy(s, d, in_sem.at[i]) for i, (s, d) in enumerate(zip(srcs, dsts))]
-    for cp in loads:
+    for cp in loads[4:]:
         cp.start()
 
     loads[0].wait()
     loads[1].wait()
     loads[2].wait()
     loads[3].wait()
-    xc[0:TOK, 0:192] = x_v[...]
-    xc[0:TOK, 192:384] = cot_v[...]
+    xc[0:TOK, 0:128] = x_v[:, 0:128]
+    xc[0:TOK, 128:256] = cot_v[:, 0:128]
+    xc[0:TOK, 256:384] = jnp.concatenate([x_v[:, 128:192], cot_v[:, 128:192]], axis=1)
     send_b[...] = mm(cells_v[0:SENT, :], xc[0:TOK, :]).astype(BF16)
-    idb[0] = jnp.zeros((16, 128), F32)
-    idb[0, 0:12, 0:24] = ids_v.reshape(12, 24)[...].astype(F32)
+    rows_id = jnp.concatenate([ids_v.reshape(12, 24)[...].astype(F32), jnp.zeros((4, 24), F32)], axis=0)
+    idb[0] = jnp.concatenate([rows_id, jnp.zeros((16, 104), F32)], axis=1).astype(BF16)
 
     pl.semaphore_wait(barrier, len(partners))
 
@@ -174,13 +175,13 @@
         return pltpu.make_async_remote_copy(
             src_ref=src, dst_ref=dst, send_sem=ss, recv_sem=rs, device_id=dev, device_id_type=MESH)
 
-    strip_to = [(lat_o, lon), (lat_o, lon), (lat, west), (lat_o, west)]
+    strip_to = [(lat_o, lon), (lat, west), (lat_o, west)]
     id_to = [(lat_o, lon), (lat, west), (lat_o, west)]
     strips = [remote(send_b.at[pl.ds(a, n)], xc.at[pl.ds(b, n)], h_ss.at[i], h_rs.at[i], strip_to[i])
               for i, (a, b, n) in enumerate(STRIPS)]
-    id_blocks = [remote(idb.at[0], idb.at[i + 1], h_ss.at[4 + i], h_rs.at[4 + i], id_to[i])
+    id_blocks = [remote(idb.at[0], idb.at[i + 1], h_ss.at[3 + i], h_rs.at[3 + i], id_to[i])
                  for i in range(3)]
-    halo = [id_blocks[0], strips[0], id_blocks[1], strips[2], id_blocks[2], strips[3], strips[1]]
+    halo = [strips[2], strips[0], strips[1]] + id_blocks
     for cp in halo:
         cp.start()
 
@@ -209,55 +210,55 @@
 
     for cp in loads[6:]:
         cp.wait()
-    wq, wk, wv = wqkv_v[:, 0:192], wqkv_v[:, 192:384], wqkv_v[:, 384:576]
     lane_head = lax.broadcasted_iota(jnp.int32, (WIN, WIDTH), 1) // 32
-    classes = lax.broadcasted_iota(jnp.int32, (WIN, 128), 1).astype(F32)
-    ones = jnp.ones((128, 128), BF16)
+    classes = lax.broadcasted_iota(jnp.int32, (TOK, 128), 1).astype(F32)
     scale = 32.0 ** (-0.5)
-
-    kept = []
+    for cp in halo:
+        cp.wait_recv()
+
+    fr = mm(moves_v[0:TOK, :], xc[...])
+    xf = jnp.concatenate([fr[:, 0:128], fr[:, 256:320]], axis=1)
+    cot_f = jnp.concatenate([fr[:, 128:256], fr[:, 320:384]], axis=1)
+    cot = cot_f.astype(BF16)
+    mean = jnp.sum(xf, axis=1, keepdims=True) * (1.0 / WIDTH)
+    xm = xf - mean
+    var = jnp.sum(xm * xm, axis=1, keepdims=True) * (1.0 / WIDTH)
+    rdev = lax.rsqrt(var + 1e-05)
+    xhat = xm * rdev
+    normed = xhat.astype(BF16)
+    q = mm(normed, wqkv_v[:, 0:192]).astype(BF16)
+    k = mm(normed, wqkv_v[:, 192:384]).astype(BF16)
+    v = mm(normed, wqkv_v[:, 384:576]).astype(BF16)
+    da = mm_nt(cot, wproj_v[...]).astype(BF16)
+
+    id_all = jnp.concatenate([idb[i] for i in range(4)], axis=0)
+    id_row = mm(idt_v[:, 0:64], id_all) * idt_v[:, 128:256].astype(F32)
+    id_cell = mm(id_row.astype(BF16), jnp.ones((128, 128), BF16))
+    key = id_cell + idt_v[:, 256:384].astype(F32) * izl.astype(F32)
+    onehot = jnp.where(key == classes, 1.0, 0.0).astype(BF16)
+
+    def spread_heads(a, heads):
+        zero = jnp.zeros((WIN, WIDTH), BF16)
+        return jnp.concatenate([jnp.where(lane_head == h, a, zero) for h in heads], axis=0)
+
+    def own_lanes(a, heads, acc):
+        for i, h in enumerate(heads):
+            part = a[i * WIN:(i + 1) * WIN]
+            acc = part if acc is None else jnp.where(lane_head == h, part, acc)
+        return acc
+
+    atts = []
     for w in range(2):
         rows = slice(w * WIN, (w + 1) * WIN)
-        if w == 0:
-            id_blocks[0].wait_recv()
-            strips[0].wait_recv()
-        else:
-            for cp in halo[2:]:
-                cp.wait_recv()
-        width, blocks = (FAR, 2) if w == 0 else (ALL, 4)
-        fr = mm(moves_v[rows, 0:width], xc[0:width, :])
-        xf = fr[:, 0:192]
-        cot_f = fr[:, 192:384]
-        cot = cot_f.astype(BF16)
-        mean = jnp.sum(xf, axis=1, keepdims=True) * (1.0 / WIDTH)
-        xm = xf - mean
-        var = jnp.sum(xm * xm, axis=1, keepdims=True) * (1.0 / WIDTH)
-        rdev = lax.rsqrt(var + 1e-05)
-        xhat = xm * rdev
-        normed = xhat.astype(BF16)
-        qw = mm(normed, wq).astype(BF16)
-        kw = mm(normed, wk).astype(BF16)
-        vw = mm(normed, wv).astype(BF16)
-        daw = mm_nt(cot, wproj_v[...]).astype(BF16)
-
-        id_all = jnp.concatenate([idb[i] for i in range(blocks)], axis=0).astype(BF16)
-        id_row = mm(idt_v[rows, 0:16 * blocks], id_all) * idt_v[rows, 128:256].astype(F32)
-        id_cell = mm(id_row.astype(BF16), ones)
-        key = id_cell + idt_v[rows, 256:384].astype(F32) * izl.astype(F32)
-        onehot = jnp.where(key == classes, 1.0, 0.0).astype(BF16)
-        block = (mm_nt(onehot, onehot) - 1.0) * 1e30
-
+        qw, kw, vw, daw = q[rows], k[rows], v[rows], da[rows]
+        block = (mm_nt(onehot[rows], onehot[rows]) - 1.0) * 1e30
         att = dq = dk = dv = None
-        for h in range(HEADS):
-            here = lane_head == h
-            zero = jnp.zeros((WIN, WIDTH), BF16)
-            qh = jnp.where(here, qw, zero)
-            kh = jnp.where(here, kw, zero)
-            vh = jnp.where(here, vw, zero)
-            dah = jnp.where(here, daw, zero)
-            hr = slice(h * WIN, (h + 1) * WIN)
+        for h0 in range(0, HEADS, STACK):
+            heads = range(h0, h0 + STACK)
+            qh, dah = spread_heads(qw, heads), spread_heads(daw, heads)
+            hr = slice(h0 * WIN, (h0 + STACK) * WIN)
             bias = jnp.concatenate([fa[hr, :], fb[hr, 0:16]], axis=1)
-            s = mm_nt(qh, kw) * scale + bias + block
+            s = mm_nt(qh, kw) * scale + bias + jnp.concatenate([block] * STACK, axis=0)
             ex = jnp.exp(s - jnp.max(s, axis=1, keepdims=True))
             p = ex * (1.0 / jnp.sum(ex, axis=1, keepdims=True))
             pb = p.astype(BF16)
@@ -265,31 +266,31 @@
             ds = p * (dp - jnp.sum(p * dp, axis=1, keepdims=True))
             dsb = ds.astype(BF16)
             ds_a = ds[:, 0:128]
-            ds_b = jnp.concatenate([ds[:, 128:144], jnp.zeros((WIN, 112), F32)], axis=1)
+            ds_b = jnp.concatenate([ds[:, 128:144], jnp.zeros((STACK * WIN, 112), F32)], axis=1)
             if w == 0:
                 ba[hr, :] = ds_a
                 bb[hr, :] = ds_b
             else:
                 ba[hr, :] += ds_a
                 bb[hr, :] += ds_b
-            terms = (mm(pb, vh), mm(dsb, kh), mm_tn(dsb, qh), mm_tn(pb, dah))
-            if h == 0:
-                att, dq, dk, dv = terms
-            else:
-                att, dq, dk, dv = att + terms[0], dq + terms[1], dk + terms[2], dv + terms[3]
-        kept.append((normed, cot, att.astype(BF16), (dq * scale).astype(BF16),
-                     (dk * scale).astype(BF16), dv.astype(BF16), cot_f, xhat, rdev))
-    normed, cot, att, dq, dk, dv, cot_f, xhat, rdev = [
-        jnp.concatenate(pair, axis=0) for pair in zip(*kept)]
-
-    gs[:, 0:192] = mm_tn(normed, dq)
-    gs[:, 192:384] = mm_tn(normed, dk)
-    gs[:, 384:576] = mm_tn(normed, dv)
-    gs[:, 576:768] = mm_tn(att, cot)
+            att = own_lanes(mm(pb, vw), heads, att)
+            dq = own_lanes(mm(dsb, kw), heads, dq)
+            dk_part, dv_part = mm_tn(dsb, qh), mm_tn(pb, dah)
+            dk = dk_part if dk is None else dk + dk_part
+            dv = dv_part if dv is None else dv + dv_part
+        atts.append(att.astype(BF16))
+        dqkv[rows, 0:192] = (dq * scale).astype(BF16)
+        dqkv[rows, 192:384] = (dk * scale).astype(BF16)
+        dqkv[rows, 384:576] = dv.astype(BF16)
+    att = jnp.concatenate(atts, axis=0)
+
+    g_qkv = mm_tn(normed, dqkv[...])
+    g_proj = mm_tn(att, cot)
+    g_mix = jnp.concatenate([g_qkv[:, 512:576], g_proj[:, 128:192]], axis=1)
+    columns = [g_qkv[:, j * 128:(j + 1) * 128] for j in range(4)] + [g_mix, g_proj[:, 0:128]]
     for i in range(ROWS_MAIN):
         for j in range(COLS_MAIN):
-            pay_m[main_place(i * COLS_MAIN + j)] = gs[
-                i * 16:(i + 1) * 16, j * 128:(j + 1) * 128].astype(BF16)
+            pay_m[main_place(i * COLS_MAIN + j)] = columns[j][i * 16:(i + 1) * 16].astype(BF16)
     for half in range(2):
         for t in range(HALF, CHUNKS * MAIN):
             pay_m[half, t // MAIN, t % MAIN] = jnp.zeros((16, 128), BF16)
@@ -327,13 +328,13 @@
             scatter.append(cp)
     ra[group] = cur[group]
 
-    dn = mm_nt(dq, wq) + mm_nt(dk, wk) + mm_nt(dv, wv)
+    dn = mm_nt(dqkv[...], wqkv_v[...])
     m1 = jnp.sum(dn, axis=1, keepdims=True) * (1.0 / WIDTH)
     m2 = jnp.sum(dn * xhat, axis=1, keepdims=True) * (1.0 / WIDTH)
     gf = (cot_f + rdev * (dn - m1 - xhat * m2)).astype(BF16)
     gback[0:TOK, :] = gf
     ret_b[...] = mm(cells_v[SENT:2 * SENT, :], gf).astype(BF16)
-    ret_to = [(lat_o, lon), (lat_o, lon), (lat, east), (lat_o, east)]
+    ret_to = [(lat_o, lon), (lat, east), (lat_o, east)]
     returns = [remote(ret_b.at[pl.ds(a, n)], gback.at[pl.ds(b, n)], r_ss.at[i], r_rs.at[i], ret_to[i])
                for i, (a, b, n) in enumerate(STRIPS)]
     for cp in returns:
@@ -386,8 +387,10 @@
         cp.wait_send()
 
 
-def unpack(field_in, fin, field_ref, gqkv_ref, gproj_ref, gbias_ref):
-    field_ref[...] = field_in[...]
+def unpack(field_in, fin, field_hbm, gqkv_hbm, gproj_hbm, gbias_hbm, gqkv_ref, gproj_ref, gbias_ref, sem):
+    outs = [(field_in, field_hbm), (gqkv_ref, gqkv_hbm), (gproj_ref, gproj_hbm), (gbias_ref, gbias_hbm)]
+    stores = [pltpu.make_async_copy(src, dst, sem.at[i]) for i, (src, dst) in enumerate(outs)]
+    stores[0].start()
     token_scale = 147456.0 ** (-0.5)
     for i in range(ROWS_MAIN):
         r = slice(i * 16, (i + 1) * 16)
@@ -395,8 +398,10 @@
         for j in range(4):
             gqkv_ref[r, j * 128:(j + 1) * 128] = row[j]
         gqkv_ref[r, 512:576] = row[4][:, 0:64]
-        gproj_ref[r, 0:64] = row[4][:, 64:128]
-        gproj_ref[r, 64:192] = row[5]
+        gproj_ref[r, 0:128] = row[5]
+        gproj_ref[r, 128:192] = row[4][:, 64:128]
+    stores[1].start()
+    stores[2].start()
     bias_rows = gbias_ref.reshape(1728, 23)
     for which in range(2):
         for j in range(3):
@@ -405,6 +410,9 @@
                 [fin[which, t // BIAS, MAIN + t % BIAS] for t in places], axis=0).astype(F32)[0:72]
             for k in range(4):
                 bias_rows[pl.ds(2 * (4 * j + k) + which, 72, stride=24), :] = roll(col, -32 * k)[:, 0:23]
+    stores[3].start()
+    for cp in stores:
+        cp.wait()
 
 
 def body(grid_state, cotangent, mask_ids, earth_bias, qkv_weight, proj_weight):
@@ -417,12 +425,12 @@
         vm((864, 2, 23), F32), vm((192, 576), BF16), vm((192, 192), BF16),
         vm((2 * SENT, TOK), BF16), vm((2 * TOK, ALL), BF16), vm((TOK, 384), BF16),
         vm((384, 1792), BF16),
-        vm((ALL, 384), BF16), vm((SENT, 384), BF16), vm((4, 16, 128), F32),
+        vm((ALL, 384), BF16), vm((SENT, 384), BF16), vm((4, 16, 128), BF16),
         vm((864, 128), F32), vm((864, 128), F32), vm((864, 128), F32), vm((864, 128), F32),
-        vm((ALL, WIDTH), BF16), vm((SENT, WIDTH), BF16), vm((192, 768), F32),
+        vm((ALL, WIDTH), BF16), vm((SENT, WIDTH), BF16), vm((TOK, 576), BF16),
         tiles(2, CHUNKS, MAIN), tiles(2, CHUNKS, BIAS), tiles(CHUNKS, MAIN), tiles(CHUNKS, BIAS),
         tiles(CHUNKS, TILES), tiles(8, TILES), tiles(8, TILES), tiles(4, TILES),
-        dma(10), dma(7), dma(7), dma(4), dma(4), dma(2), dma(2), dma(7), dma(7), dma(7), dma(7),
+        dma(10), dma(6), dma(6), dma(3), dma(3), dma(2), dma(2), dma(7), dma(7), dma(7), dma(7),
         dma(3), dma(3), dma(7), dma(7), dma(8), dma(8),
     ]
     any_space = pl.BlockSpec(memory_space=pl.ANY)
@@ -453,7 +461,8 @@
             jax.ShapeDtypeStruct((864, 2, 23), F32),
         ),
         in_specs=[in_vmem] * 2,
-        out_specs=(in_vmem,) * 4,
+        out_specs=(any_space,) * 4,
+        scratch_shapes=[vm((192, 576), F32), vm((192, 192), F32), vm((864, 2, 23), F32), dma(4)],
         compiler_params=pltpu.CompilerParams(vmem_limit_bytes=16 * 2**20),
         name="unpack",
     )(field, fin)

time: 52.8 us -> 51.3 us (0.972)
  Pallas kernels: 52 us -> 50.5 us
    pallas_call x1, Pallas kernels: 50.6 us -> 49.1 us  [body(): pl.pallas_call(kernel, out_shape=(jax.ShapeDtypeStruct((TOK, WIDTH), BF16...]
where the time goes in v4:
time: 51.3 us; the launch traced here: 51.2 us
  Pallas kernels  50.5 us (98%)
  between operations  0.64 us (1%)
    pallas_call x1, Pallas kernels, body(): pl.pallas_call(kernel, out_shape=(jax.ShapeDtypeStruct((TOK, WIDTH), BF16...  49.1 us
    pallas_call x1, Pallas kernels, body(): pl.pallas_call(unpack, out_shape=(jax.ShapeDtypeStruct((TOK, WIDTH), BF16...  1.42 us

profile of v4, /device:TPU:1, one launch (start us, length us, event | category | flops | bytes accessed | tf_op | source)
XLA Modules:
  0.0 51.2 jit_solution(16543728627890554722)
XLA Ops:
  0.6 49.1 %window_backward.1 = (bf16[288,192]{1,0:T(8,128)(2,1)S(1)}, bf16[2,8,7,16,128]{4,3,2,1,0:T(8,128)(2,1)S(1)}) custom-call(bf16[288,192]{1,0:T(8,128)(2,1)} %bitcast.11, bf16[288,192]{1,0:T(8,128)(2,1)} %bitcast.12, s32[6,2,24]{2,1,0:T(2,128)} %bitcast.13, f32[864,2,23]{2,1,0:T(2,128)} %bitcast.10, bf16[192,576]{1,0:T(8,128)(2,1)} %wqkv_hbm.1, ...), custom_call_target="tpu_custom_call" | custom-call | tf_op jit(solution)/shard_map/window_backward/pallas_call | solution.py:438
  49.7 1.4 %unpack.1 = (bf16[288,192]{1,0:T(8,128)(2,1)}, f32[192,576]{1,0:T(8,128)}, f32[192,192]{1,0:T(8,128)}, f32[864,2,23]{2,1,0:T(2,128)}) custom-call(bf16[288,192]{1,0:T(8,128)(2,1)S(1)} %get-tuple-element.10.field_in, bf16[2,8,7,16,128]{4,3,2,1,0:T(8,128)(2,1)S(1)} %get-tuple-element.11.fin), custom_call_target="tpu_custom_call" | custom-call | tf_op jit(solution)/shard_map/unpack/pallas_call | solution.py:455

commit v5 on v4

--- a/solution.py
+++ b/solution.py
@@ -18,12 +18,11 @@
 SWAP, EAST, CORNER, ALL = 288, 400, 448, 496
 STRIPS = ((0, SWAP, 112), (112, EAST, 48), (160, CORNER, 48))
 SENT = 208
-STACK = 6
-CHUNKS, TILES = 8, 7
-MAIN, BIAS = 5, 2
+CHUNKS, TILES = 8, 6
 HALF = 36
+MAIN = HALF // TILES
 ROWS_MAIN, COLS_MAIN = 12, 6
-BIAS_TILES = 15
+PACKS = (5, 5, 2)
 
 
 def build_tables():
@@ -68,7 +67,7 @@
             for y in range(12):
                 key = b * 12 + y
                 col = x * 128 + key if key < 128 else 1536 + x * 16 + key - 128
-                spread[b * 32 + x - y + 11, col] = 1
+                spread[(b // 5) * 128 + (b % 5) * 24 + x - y + 11, col] = 1
     cells = np.concatenate([send, back], axis=0)
     moves = np.concatenate([frame, out], axis=0)
     ids = np.concatenate([id_rows, np.zeros((TOK, 64), np.float32), id_cols, wrapped], axis=1)
@@ -88,7 +87,11 @@
 
 
 def main_place(t):
-    return t // HALF, (t % HALF) // MAIN, (t % HALF) % MAIN
+    return t // HALF, (t % HALF) // TILES, t % TILES
+
+
+def bias_place(t):
+    return (HALF + t) // TILES, t % TILES
 
 
 def roll(a, shift):
@@ -100,8 +103,8 @@
     x_hbm, cot_hbm, ids_hbm, eb_hbm, wqkv_hbm, wproj_hbm, cells_hbm, moves_hbm, idt_hbm, spread_hbm,
     field_ref, fin,
     x_v, cot_v, ids_v, eb_v, wqkv_v, wproj_v, cells_v, moves_v, idt_v, spread_v,
-    xc, send_b, idb, fa, fb, ba, bb, gback, ret_b, dqkv,
-    pay_m, pay_b, rc_m, rc_b, cur, ra, ry, rz,
+    xc, send_b, idb, fa, fb, ba, bb, gback, ret_b, wqkv_t,
+    pay, rc, cur, ra, ry, rz,
     in_sem, h_ss, h_rs, r_ss, r_rs, c_ss, c_rs, a_ss, a_rs, y_ss, y_rs, z_ss, z_rs,
     g_ss, g_rs, k_ss, k_rs,
 ):
@@ -192,9 +195,9 @@
     packs = []
     for g in range(3):
         acc = None
-        for k in range(4):
-            part = eb_rows[pl.ds(2 * (4 * g + k) + band, 72, stride=24), :]
-            part = roll(jnp.concatenate([part, nothing], axis=1), 32 * k)
+        for k in range(PACKS[g]):
+            part = eb_rows[pl.ds(2 * (5 * g + k) + band, 72, stride=24), :]
+            part = roll(jnp.concatenate([part, nothing], axis=1), 24 * k)
             acc = part if acc is None else acc + part
         packs.append(acc)
     e = jnp.concatenate(packs, axis=1)
@@ -210,6 +213,7 @@
 
     for cp in loads[6:]:
         cp.wait()
+    wqkv_t[...] = wqkv_v[...].astype(F32).T.astype(BF16)
     lane_head = lax.broadcasted_iota(jnp.int32, (WIN, WIDTH), 1) // 32
     classes = lax.broadcasted_iota(jnp.int32, (TOK, 128), 1).astype(F32)
     scale = 32.0 ** (-0.5)
@@ -227,8 +231,6 @@
     xhat = xm * rdev
     normed = xhat.astype(BF16)
     q = mm(normed, wqkv_v[:, 0:192]).astype(BF16)
-    k = mm(normed, wqkv_v[:, 192:384]).astype(BF16)
-    v = mm(normed, wqkv_v[:, 384:576]).astype(BF16)
     da = mm_nt(cot, wproj_v[...]).astype(BF16)
 
     id_all = jnp.concatenate([idb[i] for i in range(4)], axis=0)
@@ -237,64 +239,54 @@
     key = id_cell + idt_v[:, 256:384].astype(F32) * izl.astype(F32)
     onehot = jnp.where(key == classes, 1.0, 0.0).astype(BF16)
 
-    def spread_heads(a, heads):
+    def spread_heads(a):
         zero = jnp.zeros((WIN, WIDTH), BF16)
-        return jnp.concatenate([jnp.where(lane_head == h, a, zero) for h in heads], axis=0)
-
-    def own_lanes(a, heads, acc):
-        for i, h in enumerate(heads):
-            part = a[i * WIN:(i + 1) * WIN]
-            acc = part if acc is None else jnp.where(lane_head == h, part, acc)
-        return acc
-
-    atts = []
+        return jnp.concatenate([jnp.where(lane_head == h, a, zero) for h in range(HEADS)], axis=0)
+
+    def each_head(dot, a, b):
+        parts = [dot(a[h * 32:(h + 1) * 32], b[h * WIN:(h + 1) * WIN]) for h in range(HEADS)]
+        return jnp.concatenate(parts, axis=0)
+
+    g_qkv = g_proj = None
+    d_qkv_t = []
     for w in range(2):
         rows = slice(w * WIN, (w + 1) * WIN)
-        qw, kw, vw, daw = q[rows], k[rows], v[rows], da[rows]
+        normed_t = xhat[rows].T.astype(BF16)
+        qkv_t = mm_nt(wqkv_t[...], normed[rows]).astype(BF16)
+        q_t, k_t, v_t = qkv_t[0:192], qkv_t[192:384], qkv_t[384:576]
+        da_t = mm_nt(wproj_v[...], cot[rows]).astype(BF16)
         block = (mm_nt(onehot[rows], onehot[rows]) - 1.0) * 1e30
-        att = dq = dk = dv = None
-        for h0 in range(0, HEADS, STACK):
-            heads = range(h0, h0 + STACK)
-            qh, dah = spread_heads(qw, heads), spread_heads(daw, heads)
-            hr = slice(h0 * WIN, (h0 + STACK) * WIN)
-            bias = jnp.concatenate([fa[hr, :], fb[hr, 0:16]], axis=1)
-            s = mm_nt(qh, kw) * scale + bias + jnp.concatenate([block] * STACK, axis=0)
-            ex = jnp.exp(s - jnp.max(s, axis=1, keepdims=True))
-            p = ex * (1.0 / jnp.sum(ex, axis=1, keepdims=True))
-            pb = p.astype(BF16)
-            dp = mm_nt(dah, vw)
-            ds = p * (dp - jnp.sum(p * dp, axis=1, keepdims=True))
-            dsb = ds.astype(BF16)
-            ds_a = ds[:, 0:128]
-            ds_b = jnp.concatenate([ds[:, 128:144], jnp.zeros((STACK * WIN, 112), F32)], axis=1)
-            if w == 0:
-                ba[hr, :] = ds_a
-                bb[hr, :] = ds_b
-            else:
-                ba[hr, :] += ds_a
-                bb[hr, :] += ds_b
-            att = own_lanes(mm(pb, vw), heads, att)
-            dq = own_lanes(mm(dsb, kw), heads, dq)
-            dk_part, dv_part = mm_tn(dsb, qh), mm_tn(pb, dah)
-            dk = dk_part if dk is None else dk + dk_part
-            dv = dv_part if dv is None else dv + dv_part
-        atts.append(att.astype(BF16))
-        dqkv[rows, 0:192] = (dq * scale).astype(BF16)
-        dqkv[rows, 192:384] = (dk * scale).astype(BF16)
-        dqkv[rows, 384:576] = dv.astype(BF16)
-    att = jnp.concatenate(atts, axis=0)
-
-    g_qkv = mm_tn(normed, dqkv[...])
-    g_proj = mm_tn(att, cot)
+        bias = jnp.concatenate([fa[...], fb[:, 0:16]], axis=1)
+        s = mm(spread_heads(q[rows]), k_t) * scale + bias + jnp.concatenate([block] * HEADS, axis=0)
+        ex = jnp.exp(s - jnp.max(s, axis=1, keepdims=True))
+        p = ex * (1.0 / jnp.sum(ex, axis=1, keepdims=True))
+        pb = p.astype(BF16)
+        dp = mm(spread_heads(da[rows]), v_t)
+        ds = p * (dp - jnp.sum(p * dp, axis=1, keepdims=True))
+        dsb = ds.astype(BF16)
+        ds_a = ds[:, 0:128]
+        ds_b = jnp.concatenate([ds[:, 128:144], jnp.zeros((HEADS * WIN, 112), F32)], axis=1)
+        if w == 0:
+            ba[...] = ds_a
+            bb[...] = ds_b
+        else:
+            ba[...] += ds_a
+            bb[...] += ds_b
+        att_t = each_head(mm_nt, v_t, pb).astype(BF16)
+        dq_t = (each_head(mm_nt, k_t, dsb) * scale).astype(BF16)
+        dk_t = (each_head(mm, q_t, dsb) * scale).astype(BF16)
+        dv_t = each_head(mm, da_t, pb).astype(BF16)
+        d_qkv_t.append(jnp.concatenate([dq_t, dk_t, dv_t], axis=0))
+        w_qkv, w_proj = mm_nt(normed_t, d_qkv_t[w]), mm(att_t, cot[rows])
+        g_qkv = w_qkv if w == 0 else g_qkv + w_qkv
+        g_proj = w_proj if w == 0 else g_proj + w_proj
+
     g_mix = jnp.concatenate([g_qkv[:, 512:576], g_proj[:, 128:192]], axis=1)
     columns = [g_qkv[:, j * 128:(j + 1) * 128] for j in range(4)] + [g_mix, g_proj[:, 0:128]]
     for i in range(ROWS_MAIN):
         for j in range(COLS_MAIN):
-            pay_m[main_place(i * COLS_MAIN + j)] = columns[j][i * 16:(i + 1) * 16].astype(BF16)
-    for half in range(2):
-        for t in range(HALF, CHUNKS * MAIN):
-            pay_m[half, t // MAIN, t % MAIN] = jnp.zeros((16, 128), BF16)
-    cores = [remote(pay_m.at[1 - core], rc_m, c_ss.at[0], c_rs.at[0], sibling)]
+            pay[main_place(i * COLS_MAIN + j)] = columns[j][i * 16:(i + 1) * 16].astype(BF16)
+    cores = [remote(pay.at[1 - core, pl.ds(0, MAIN)], rc.at[pl.ds(0, MAIN)], c_ss.at[0], c_rs.at[0], sibling)]
     cores[0].start()
 
     mains, tails = [], [None, None]
@@ -306,29 +298,29 @@
     t_hi = terms.astype(BF16)
     t_lo = (terms - t_hi.astype(F32)).astype(BF16)
     gb = mm_nt(t_hi, spread_v[...]) + mm_nt(t_lo, spread_v[...])
-    gb = jnp.concatenate([gb, jnp.zeros((8, 384), F32)], axis=0)
+    g0, g1, g2 = gb[:, 0:128], gb[:, 128:256], gb[:, 256:384]
+    rest = jnp.concatenate([roll(g2[40:72], 64), jnp.zeros((8, 128), F32)], axis=0)
+    packed = jnp.concatenate([g0, g1[64:72], g1[0:64], g2[0:40] + rest, jnp.zeros((8, 128), F32)], axis=0)
     for which in range(2):
-        mine = jnp.where(band == which, gb, 0.0).astype(BF16)
-        for t in range(BIAS_TILES):
-            i, j = t // 3, t % 3
-            pay_b[which, t // BIAS, t % BIAS] = mine[i * 16:(i + 1) * 16, j * 128:(j + 1) * 128]
-        pay_b[which, CHUNKS - 1, BIAS - 1] = jnp.zeros((16, 128), BF16)
-    cores.append(remote(pay_b.at[1 - core], rc_b, c_ss.at[1], c_rs.at[1], sibling))
+        mine = jnp.where(band == which, packed, 0.0).astype(BF16)
+        for t in range(12):
+            pay[(which, *bias_place(t))] = mine[t * 16:(t + 1) * 16]
+    rest_of = pl.ds(MAIN, CHUNKS - MAIN)
+    cores.append(remote(pay.at[1 - core, rest_of], rc.at[rest_of], c_ss.at[1], c_rs.at[1], sibling))
     cores[1].start()
 
     for cp in cores:
         cp.wait_recv()
     scatter = []
     for d, j in enumerate(to_first + [group]):
-        cur[j, 0:MAIN] = (pay_m[core, j].astype(F32) + rc_m[j].astype(F32)).astype(BF16)
-        cur[j, MAIN:TILES] = (pay_b[core, j].astype(F32) + rc_b[j].astype(F32)).astype(BF16)
+        cur[j] = (pay[core, j].astype(F32) + rc[j].astype(F32)).astype(BF16)
         if d < 7:
             cp = remote(cur.at[j], ra.at[group], a_ss.at[d], a_rs.at[d], member(j))
             cp.start()
             scatter.append(cp)
     ra[group] = cur[group]
 
-    dn = mm_nt(dqkv[...], wqkv_v[...])
+    dn = jnp.concatenate([mm_tn(d, wqkv_t[...]) for d in d_qkv_t], axis=0)
     m1 = jnp.sum(dn, axis=1, keepdims=True) * (1.0 / WIDTH)
     m2 = jnp.sum(dn * xhat, axis=1, keepdims=True) * (1.0 / WIDTH)
     gf = (cot_f + rdev * (dn - m1 - xhat * m2)).astype(BF16)
@@ -404,12 +396,14 @@
     stores[2].start()
     bias_rows = gbias_ref.reshape(1728, 23)
     for which in range(2):
-        for j in range(3):
-            places = [i * 3 + j for i in range(5)]
-            col = jnp.concatenate(
-                [fin[which, t // BIAS, MAIN + t % BIAS] for t in places], axis=0).astype(F32)[0:72]
-            for k in range(4):
-                bias_rows[pl.ds(2 * (4 * j + k) + which, 72, stride=24), :] = roll(col, -32 * k)[:, 0:23]
+        packed = jnp.concatenate([fin[(which, *bias_place(t))] for t in range(12)], axis=0).astype(F32)
+        rest = packed[144:184]
+        cols = [packed[0:72], jnp.concatenate([packed[80:144], packed[72:80]], axis=0),
+                jnp.concatenate([rest, roll(rest[0:32], -64)], axis=0)]
+        for g in range(3):
+            for k in range(PACKS[g]):
+                place = pl.ds(2 * (5 * g + k) + which, 72, stride=24)
+                bias_rows[place, :] = roll(cols[g], -24 * k)[:, 0:23]
     stores[3].start()
     for cp in stores:
         cp.wait()
@@ -427,9 +421,8 @@
         vm((384, 1792), BF16),
         vm((ALL, 384), BF16), vm((SENT, 384), BF16), vm((4, 16, 128), BF16),
         vm((864, 128), F32), vm((864, 128), F32), vm((864, 128), F32), vm((864, 128), F32),
-        vm((ALL, WIDTH), BF16), vm((SENT, WIDTH), BF16), vm((TOK, 576), BF16),
-        tiles(2, CHUNKS, MAIN), tiles(2, CHUNKS, BIAS), tiles(CHUNKS, MAIN), tiles(CHUNKS, BIAS),
-        tiles(CHUNKS, TILES), tiles(8, TILES), tiles(8, TILES), tiles(4, TILES),
+        vm((ALL, WIDTH), BF16), vm((SENT, WIDTH), BF16), vm((576, WIDTH), BF16),
+        tiles(2, CHUNKS, TILES), tiles(CHUNKS, TILES), tiles(CHUNKS, TILES), tiles(8, TILES), tiles(8, TILES), tiles(4, TILES),
         dma(10), dma(6), dma(6), dma(3), dma(3), dma(2), dma(2), dma(7), dma(7), dma(7), dma(7),
         dma(3), dma(3), dma(7), dma(7), dma(8), dma(8),
     ]

time: 51.3 us -> 50.4 us (0.982)
  Pallas kernels: 50.5 us -> 49.6 us
    pallas_call x1, Pallas kernels: 49.1 us -> 48.2 us  [body(): pl.pallas_call(kernel, out_shape=(jax.ShapeDtypeStruct((TOK, WIDTH), BF16...]
where the time goes in v5:
time: 50.4 us; the launch traced here: 50.3 us
  Pallas kernels  49.6 us (98%)
  between operations  0.64 us (1%)
    pallas_call x1, Pallas kernels, body(): pl.pallas_call(kernel, out_shape=(jax.ShapeDtypeStruct((TOK, WIDTH), BF16...  48.2 us
    pallas_call x1, Pallas kernels, body(): pl.pallas_call(unpack, out_shape=(jax.ShapeDtypeStruct((TOK, WIDTH), BF16...  1.44 us

profile of v5, /device:TPU:1, one launch (start us, length us, event | category | flops | bytes accessed | tf_op | source)
XLA Modules:
  0.0 50.3 jit_solution(16273776828401635560)
XLA Ops:
  0.6 48.2 %window_backward.1 = (bf16[288,192]{1,0:T(8,128)(2,1)S(1)}, bf16[2,8,6,16,128]{4,3,2,1,0:T(8,128)(2,1)S(1)}) custom-call(bf16[288,192]{1,0:T(8,128)(2,1)} %bitcast.11, bf16[288,192]{1,0:T(8,128)(2,1)} %bitcast.12, s32[6,2,24]{2,1,0:T(2,128)} %bitcast.13, f32[864,2,23]{2,1,0:T(2,128)} %bitcast.10, bf16[192,576]{1,0:T(8,128)(2,1)} %wqkv_hbm.1, ...), custom_call_target="tpu_custom_call" | custom-call | tf_op jit(solution)/shard_map/window_backward/pallas_call | solution.py:431
  48.8 1.4 %unpack.1 = (bf16[288,192]{1,0:T(8,128)(2,1)}, f32[192,576]{1,0:T(8,128)}, f32[192,192]{1,0:T(8,128)}, f32[864,2,23]{2,1,0:T(2,128)}) custom-call(bf16[288,192]{1,0:T(8,128)(2,1)S(1)} %get-tuple-element.10.field_in, bf16[2,8,6,16,128]{4,3,2,1,0:T(8,128)(2,1)S(1)} %get-tuple-element.11.fin), custom_call_target="tpu_custom_call" | custom-call | tf_op jit(solution)/shard_map/unpack/pallas_call | solution.py:448

commit v6 on v5

--- a/solution.py
+++ b/solution.py
@@ -22,6 +22,7 @@
 HALF = 36
 MAIN = HALF // TILES
 ROWS_MAIN, COLS_MAIN = 12, 6
+PAD = 880
 PACKS = (5, 5, 2)
 
 
@@ -146,7 +147,7 @@
 
     srcs = [x_hbm, cot_hbm, cells_hbm, ids_hbm, eb_hbm, spread_hbm, moves_hbm, idt_hbm,
             wqkv_hbm, wproj_hbm]
-    dsts = [x_v, cot_v, cells_v, ids_v, eb_v, spread_v, moves_v, idt_v, wqkv_v, wproj_v]
+    dsts = [x_v, cot_v, cells_v, ids_v, eb_v.at[pl.ds(0, 864)], spread_v, moves_v, idt_v, wqkv_v, wproj_v]
     loads = [pltpu.make_async_copy(s, d, in_sem.at[i]) for i, (s, d) in enumerate(zip(srcs, dsts))]
     for cp in loads[:4]:
         cp.start()
@@ -190,7 +191,7 @@
 
     loads[4].wait()
     loads[5].wait()
-    eb_rows = eb_v.reshape(1728, 23)
+    eb_rows = eb_v.reshape(2 * PAD, 23)
     nothing = jnp.zeros((72, 105), F32)
     packs = []
     for g in range(3):
@@ -256,7 +257,7 @@
         q_t, k_t, v_t = qkv_t[0:192], qkv_t[192:384], qkv_t[384:576]
         da_t = mm_nt(wproj_v[...], cot[rows]).astype(BF16)
         block = (mm_nt(onehot[rows], onehot[rows]) - 1.0) * 1e30
-        bias = jnp.concatenate([fa[...], fb[:, 0:16]], axis=1)
+        bias = jnp.concatenate([fa[0:864, :], fb[0:864, 0:16]], axis=1)
         s = mm(spread_heads(q[rows]), k_t) * scale + bias + jnp.concatenate([block] * HEADS, axis=0)
         ex = jnp.exp(s - jnp.max(s, axis=1, keepdims=True))
         p = ex * (1.0 / jnp.sum(ex, axis=1, keepdims=True))
@@ -267,11 +268,11 @@
         ds_a = ds[:, 0:128]
         ds_b = jnp.concatenate([ds[:, 128:144], jnp.zeros((HEADS * WIN, 112), F32)], axis=1)
         if w == 0:
-            ba[...] = ds_a
-            bb[...] = ds_b
+            ba[0:864, :] = ds_a
+            bb[0:864, :] = ds_b
         else:
-            ba[...] += ds_a
-            bb[...] += ds_b
+            ba[0:864, :] += ds_a
+            bb[0:864, :] += ds_b
         att_t = each_head(mm_nt, v_t, pb).astype(BF16)
         dq_t = (each_head(mm_nt, k_t, dsb) * scale).astype(BF16)
         dk_t = (each_head(mm, q_t, dsb) * scale).astype(BF16)
@@ -380,7 +381,7 @@
 
 
 def unpack(field_in, fin, field_hbm, gqkv_hbm, gproj_hbm, gbias_hbm, gqkv_ref, gproj_ref, gbias_ref, sem):
-    outs = [(field_in, field_hbm), (gqkv_ref, gqkv_hbm), (gproj_ref, gproj_hbm), (gbias_ref, gbias_hbm)]
+    outs = [(field_in, field_hbm), (gqkv_ref, gqkv_hbm), (gproj_ref, gproj_hbm), (gbias_ref.at[pl.ds(0, 864)], gbias_hbm)]
     stores = [pltpu.make_async_copy(src, dst, sem.at[i]) for i, (src, dst) in enumerate(outs)]
     stores[0].start()
     token_scale = 147456.0 ** (-0.5)
@@ -394,7 +395,7 @@
         gproj_ref[r, 128:192] = row[4][:, 64:128]
     stores[1].start()
     stores[2].start()
-    bias_rows = gbias_ref.reshape(1728, 23)
+    bias_rows = gbias_ref.reshape(2 * PAD, 23)
     for which in range(2):
         packed = jnp.concatenate([fin[(which, *bias_place(t))] for t in range(12)], axis=0).astype(F32)
         rest = packed[144:184]
@@ -416,11 +417,11 @@
     tiles = lambda *n: vm((*n, 16, 128), BF16)
     scratch = [
         vm((TOK, WIDTH), BF16), vm((TOK, WIDTH), BF16), vm((6, 2, 24), jnp.int32),
-        vm((864, 2, 23), F32), vm((192, 576), BF16), vm((192, 192), BF16),
+        vm((PAD, 2, 23), F32), vm((192, 576), BF16), vm((192, 192), BF16),
         vm((2 * SENT, TOK), BF16), vm((2 * TOK, ALL), BF16), vm((TOK, 384), BF16),
         vm((384, 1792), BF16),
         vm((ALL, 384), BF16), vm((SENT, 384), BF16), vm((4, 16, 128), BF16),
-        vm((864, 128), F32), vm((864, 128), F32), vm((864, 128), F32), vm((864, 128), F32),
+        vm((PAD, 128), F32), vm((PAD, 128), F32), vm((PAD, 128), F32), vm((PAD, 128), F32),
         vm((ALL, WIDTH), BF16), vm((SENT, WIDTH), BF16), vm((576, WIDTH), BF16),
         tiles(2, CHUNKS, TILES), tiles(CHUNKS, TILES), tiles(CHUNKS, TILES), tiles(8, TILES), tiles(8, TILES), tiles(4, TILES),
         dma(10), dma(6), dma(6), dma(3), dma(3), dma(2), dma(2), dma(7), dma(7), dma(7), dma(7),
@@ -455,7 +456,7 @@
         ),
         in_specs=[in_vmem] * 2,
         out_specs=(any_space,) * 4,
-        scratch_shapes=[vm((192, 576), F32), vm((192, 192), F32), vm((864, 2, 23), F32), dma(4)],
+        scratch_shapes=[vm((192, 576), F32), vm((192, 192), F32), vm((PAD, 2, 23), F32), dma(4)],
         compiler_params=pltpu.CompilerParams(vmem_limit_bytes=16 * 2**20),
         name="unpack",
     )(field, fin)

time: 50.4 us -> 50.4 us (level)
  no operation moved by 1% of the time
where the time goes in v6:
time: 50.4 us; the launch traced here: 50.3 us
  Pallas kernels  49.6 us (98%)
  between operations  0.64 us (1%)
    pallas_call x1, Pallas kernels, body(): pl.pallas_call(kernel, out_shape=(jax.ShapeDtypeStruct((TOK, WIDTH), BF16...  48.2 us
    pallas_call x1, Pallas kernels, body(): pl.pallas_call(unpack, out_shape=(jax.ShapeDtypeStruct((TOK, WIDTH), BF16...  1.44 us

profile of v6, /device:TPU:1, one launch (start us, length us, event | category | flops | bytes accessed | tf_op | source)
XLA Modules:
  0.0 50.3 jit_solution(9943387143976715570)
XLA Ops:
  0.6 48.2 %window_backward.1 = (bf16[288,192]{1,0:T(8,128)(2,1)S(1)}, bf16[2,8,6,16,128]{4,3,2,1,0:T(8,128)(2,1)S(1)}) custom-call(bf16[288,192]{1,0:T(8,128)(2,1)} %bitcast.11, bf16[288,192]{1,0:T(8,128)(2,1)} %bitcast.12, s32[6,2,24]{2,1,0:T(2,128)} %bitcast.13, f32[864,2,23]{2,1,0:T(2,128)} %bitcast.10, bf16[192,576]{1,0:T(8,128)(2,1)} %wqkv_hbm.1, ...), custom_call_target="tpu_custom_call" | custom-call | tf_op jit(solution)/shard_map/window_backward/pallas_call | solution.py:432
  48.8 1.4 %unpack.1 = (bf16[288,192]{1,0:T(8,128)(2,1)}, f32[192,576]{1,0:T(8,128)}, f32[192,192]{1,0:T(8,128)}, f32[864,2,23]{2,1,0:T(2,128)}) custom-call(bf16[288,192]{1,0:T(8,128)(2,1)S(1)} %get-tuple-element.10.field_in, bf16[2,8,6,16,128]{4,3,2,1,0:T(8,128)(2,1)S(1)} %get-tuple-element.11.fin), custom_call_target="tpu_custom_call" | custom-call | tf_op jit(solution)/shard_map/unpack/pallas_call | solution.py:449
